TPU v7x, 128 devices: a whole 4x4x4 slice. The times are simulated.
128 devices in a mesh: dp: 16 (over x_hi, z, core), tensor: 8 (over y, x_lo).
Axes of the slice: x: 4 (x_hi: 2, x_lo: 2; x = x_hi * 2 + x_lo), y: 4, z: 4, core: 2. Of those that a mesh axis runs over, the one named last changes fastest.
Arguments:
- teacher_hidden: bfloat16 [8192, 7168], P('dp', 'tensor'), may hold values from -6 to 6
- teacher_down: bfloat16 [7168, 5120], P('tensor'), may hold values from -0.0625 to 0.0625
- student_in: bfloat16 [8192, 4096], P(('dp', 'tensor')), may hold values from -6 to 6
- student_weight: bfloat16 [4096, 4096], P('dp', 'tensor'), may hold values from -0.09375 to 0.09375
- projection: bfloat16 [5120, 4096], P('dp', 'tensor'), may hold values from -0.078125 to 0.078125
Outputs:
- grad_weight: float32 [4096, 4096], P('dp', 'tensor')
- grad_projection: float32 [5120, 4096], P('dp', 'tensor')
All inputs are finite; a program needn't handle non-finite values.
Results may differ from a plain program's by a relative error of at most 0.003.
Values may be sent and summed in bfloat16 or wider, within the bound.
A program may use at most 128 MiB of HBM per device.

v0:
```python
import math

import jax
import jax.numpy as jnp
from jax import lax
from jax.sharding import PartitionSpec as P


def contract_rows(left, right):
    return lax.dot_general(
        left, right, (((0,), (0,)), ((), ())), preferred_element_type=jnp.float32
    )


def on_device(teacher_hidden, teacher_down, student_in, student_weight, projection):
    partial_value = jnp.dot(teacher_hidden, teacher_down, preferred_element_type=jnp.float32)
    teacher_out = lax.psum(partial_value, "tensor").astype(jnp.bfloat16)
    group_input = lax.all_gather(student_in, "tensor", axis=0, tiled=True)
    group_rows = group_input.shape[0]
    inputs = group_input
    student_out = jnp.dot(
        inputs,
        lax.all_gather(student_weight, "dp", axis=0, tiled=True),
        preferred_element_type=jnp.float32,
    )
    inputs = teacher_out
    target = jnp.dot(
        inputs,
        lax.all_gather(projection, "dp", axis=0, tiled=True),
        preferred_element_type=jnp.float32,
    )
    residual = (student_out - target).astype(jnp.bfloat16)
    total_rows = group_rows * lax.axis_size("dp")
    factor = 1.0 / math.sqrt(total_rows)
    inputs = group_input
    grad_weight = lax.psum_scatter(
        contract_rows(inputs, residual), "dp", scatter_dimension=0, tiled=True
    )
    inputs = teacher_out
    grad_projection = lax.psum_scatter(
        contract_rows(inputs, residual), "dp", scatter_dimension=0, tiled=True
    )
    return (grad_weight * factor, grad_projection * factor)


def solution(mesh):
    in_specs = (
        P("dp", "tensor"),
        P("tensor", None),
        P(("dp", "tensor"), None),
        P("dp", "tensor"),
        P("dp", "tensor"),
    )
    out_specs = (P("dp", "tensor"), P("dp", "tensor"))
    return jax.shard_map(
        on_device, mesh=mesh, in_specs=in_specs, out_specs=out_specs, check_vma=False
    )
```

profile of v0, /device:TPU:1, one launch (start us, length us, event | category | flops | bytes accessed | tf_op | source)
XLA Modules:
  0.0 776.6 jit_solution(4665317202825300464)
XLA Ops:
  7.2 0.0 copy-start
  7.2 0.0 all-gather.4.cloned.1.call-start
  7.2 0.7 all-gather.4.cloned.1.call-update
  7.9 0.0 all-gather.6.cloned.1.call-start
  8.0 0.7 all-gather.6.cloned.1.call-update
  8.7 0.0 all-gather.8.cloned.1.call-start
  8.7 0.7 all-gather.8.cloned.1.call-update
  9.4 0.0 reduce-scatter.3.cloned.1.call-start
  9.4 0.0 copy-done
  9.5 11.7 %fusion.11 = f32[512,5120]{1,0:T(8,128)} fusion(bf16[512,896]{1,0:T(8,128)(2,1)S(1)} %copy-done, bf16[896,5120]{1,0:T(8,128)(2,1)} %param.6), kind=kOutput, calls=%fused_computation.10 | convolution fusion | flops 4697620480 | bytes 20578304 | tf_op jit(solution)/shard_map/dot_general | solution.py:16
  21.1 509.3 %all-reduce.1 = bf16[512,5120]{1,0:T(8,128)(2,1)} all-reduce(f32[512,5120]{1,0:T(8,128)} %fusion.11), channel_id=1, replica_groups=mesh['dp'=16,'tensor'=8] {'tensor'}, use_global_device_ids=true, to_apply=%region_0.0 | all-reduce | flops 2621440 | bytes 15728640 | tf_op jit(solution)/shard_map/psum | solution.py:17
  530.4 5.8 fusion.10
  536.2 0.0 all-gather.8.cloned.1.call-done
  536.3 7.1 fusion.7
  543.3 5.7 convolution_bitcast_fusion
  549.0 0.0 reduce-scatter.3.cloned.1.call-update
  549.1 0.0 reduce-scatter.5.cloned.1.call-start
  549.1 8.1 %fusion.12 = f32[5120,512]{1,0:T(8,128)} fusion(bf16[512,5120]{1,0:T(8,128)(2,1)} %all-reduce.1, bf16[512,512]{1,0:T(8,128)(2,1)S(1)} %fusion.7), kind=kOutput, calls=%fused_computation.11 | convolution fusion | flops 2684354560 | bytes 16252928 | tf_op jit(solution)/shard_map/dot_general | solution.py:10
  557.2 0.0 reduce-scatter.5.cloned.1.call-update
  557.2 95.3 %reduce-scatter.3.cloned.1.call-done = f32[256,512]{0,1:T(8,128)} async-done(((f32[4096,512]{0,1:T(8,128)}), f32[256,512]{0,1:T(8,128)}) %reduce-scatter.3.cloned.1.call-update) | async-done | bytes 524304 | tf_op jit(solution)/shard_map/reduce_scatter | solution.py:36
  652.5 1.1 broadcast_multiply_fusion.1
  653.6 1.0 copy.7
  654.6 113.5 %reduce-scatter.5.cloned.1.call-done = f32[320,512]{1,0:T(8,128)} async-done(((f32[5120,512]{1,0:T(8,128)}), f32[320,512]{1,0:T(8,128)}) %reduce-scatter.5.cloned.1.call-update) | async-done | bytes 655376 | tf_op jit(solution)/shard_map/reduce_scatter | solution.py:40
  768.1 2.0 broadcast_multiply_fusion
  (4 shorter events, 0.0 us)
Async XLA Ops:
  7.2 2.3 copy-start
  7.2 523.2 %all-gather.4.cloned.1.call-start = ((), (), s32[]{:S(2)}) async-start(), calls=%async_computation.2 | async-start | bytes 4718592 | tf_op jit(solution)/shard_map/all_gather | solution.py:18
  7.9 522.5 %all-gather.6.cloned.1.call-start = ((), (), s32[]{:S(2)}) async-start(), calls=%async_computation.3 | async-start | bytes 4456448 | tf_op jit(solution)/shard_map/all_gather | solution.py:23
  8.7 527.6 %all-gather.8.cloned.1.call-start = ((), (), s32[]{:S(2)}) async-start(), calls=%async_computation.4 | async-start | bytes 5570560 | tf_op jit(solution)/shard_map/all_gather | solution.py:29
  9.4 643.1 %reduce-scatter.3.cloned.1.call-start = ((), (), s32[]{:S(2)}) async-start(), calls=%async_computation.5 | async-start | bytes 8912896 | tf_op jit(solution)/shard_map/reduce_scatter | solution.py:36
  536.3 7.1 copy-start.1
  549.1 219.0 %reduce-scatter.5.cloned.1.call-start = ((), (), s32[]{:S(2)}) async-start(), calls=%async_computation.6 | async-start | bytes 11141120 | tf_op jit(solution)/shard_map/reduce_scatter | solution.py:40
Sparse Core Ops, SparseCore 0:
  9.7 164.6 all-gather.3
  176.8 70.9 all-gather.5
  250.3 75.5 all-gather.7
  549.2 103.2 reduce-scatter.2
  656.7 111.4 reduce-scatter.4
where the time goes:
time: 777 us
  blocking collectives  509 us (66%)
  waiting for transfers between devices  211 us (27%)
  matrix products  38.3 us (5%)
  between operations  13.8 us (2%)
    psum x1, blocking collectives, on_device(): teacher_out = lax.psum(partial_value, 'tensor').astype(jnp.bfloat16)  509 us
    reduce_scatter x2, waiting for transfers between devices, on_device(): lax.psum_scatter(contract_rows(inputs, residual), 'dp', scatter_dimension...  209 us
  transfers between devices with their start and end apart: 5, of which 2 were waited for; matrix products, arithmetic and copies ran while one was open for 4% of the time, Pallas kernels for 0%

commit v1 on v0

v1 whole, which is shorter than its diff:
```python
import functools
import math

import jax
import jax.numpy as jnp
from jax import lax
from jax.experimental import pallas as pl
from jax.experimental.pallas import tpu as pltpu
from jax.sharding import PartitionSpec as P

MESH = pl.DeviceIdType.MESH
BF16 = jnp.bfloat16
F32 = jnp.float32


class Place:
    def __init__(self):
        self.d = lax.axis_index("dp")
        self.t = lax.axis_index("tensor")
        self.core = lax.rem(self.d, 2)
        self.q = lax.div(self.d, 2)
        self.z = lax.rem(self.q, 4)
        self.xh = lax.div(self.q, 4)
        self.y = lax.div(self.t, 2)
        self.xl = lax.rem(self.t, 2)

    def dev(self, dy=0, dx=0, dz=0, dh=0, dc=0):
        d = self.dp(dz, dh, dc)
        return (d, self.tensor(dy, dx))

    def tensor(self, dy=0, dx=0):
        return lax.rem(self.y + dy + 4, 4) * 2 + lax.rem(self.xl + dx, 2)

    def chip(self, dz=0, dh=0):
        return lax.rem(self.xh + dh, 2) * 4 + lax.rem(self.z + dz + 4, 4)

    def dp(self, dz=0, dh=0, dc=0):
        return self.chip(dz, dh) * 2 + lax.rem(self.core + dc, 2)


class Copies:
    def __init__(self, send, recv, local):
        self.send, self.recv, self.local = send, recv, local
        self.n = 0
        self.m = 0
        self.sent = []
        self.kept = []

    def remote(self, src, dst, to):
        c = pltpu.make_async_remote_copy(
            src_ref=src,
            dst_ref=dst,
            send_sem=self.send.at[self.n],
            recv_sem=self.recv.at[self.n],
            device_id=to,
            device_id_type=MESH,
        )
        self.n += 1
        c.start()
        self.sent.append(c)
        return c

    def keep(self, src, dst):
        c = pltpu.make_async_copy(src, dst, self.local.at[self.m])
        self.m += 1
        c.start()
        self.kept.append(c)
        return c

    def drain(self):
        for c in self.kept:
            c.wait()
        for c in self.sent:
            c.wait_send()


def barrier(devices):
    sem = pltpu.get_barrier_semaphore()
    for dev in devices:
        pl.semaphore_signal(sem, inc=1, device_id=dev, device_id_type=MESH)
    pl.semaphore_wait(sem, len(devices))


def columns(index, width):
    return pl.ds(pl.multiple_of(index * width, 128), width)


def gather_tensor(cp, me, own, place, cut):
    first = {}
    first["x0"] = cp.remote(own(0), place(me.t, 0), me.dev(dx=1))
    for k in (1, 3, 2):
        first["y1", k] = cp.remote(own(1), place(me.t, 1), me.dev(dy=k))
    for k in (1, 3, 2):
        first["y0", k] = cp.remote(own(0), place(me.t, 0), me.dev(dy=k))
    first["x1"] = cp.remote(own(1), place(me.t, 1), me.dev(dx=1))
    second = {}

    def forward():
        first["x0"].wait_recv()
        tx = me.tensor(dx=1)
        for k in (1, 3, 2):
            second["y", k] = cp.remote(place(tx, 0), place(tx, 0), me.dev(dy=k))
        for k in (1, 3, 2):
            first["y1", k].wait_recv()
            ty = me.tensor(dy=-k)
            second["x", k] = cp.remote(place(ty, 1), place(ty, 1), me.dev(dx=1))

    def finish(done):
        for k in (1, 3, 2):
            first["y0", k].wait_recv()
            done(me.tensor(dy=-k))
        first["x1"].wait_recv()
        done(me.tensor(dx=1))
        for k in (1, 3, 2):
            second["y", k].wait_recv()
            second["x", k].wait_recv()
            done(me.tensor(dy=-k, dx=1))

    return forward, finish


def nothing(t):
    return None


def hidden_and_down(h, d, hh, dd, send, recv, local):
    me = Place()
    cp = Copies(send, recv, local)
    piece = me.z * 2 + me.core
    tensor_peers = [me.dev(dy=a, dx=b) for a in range(4) for b in range(2) if a or b]
    z_peers = [me.dev(dz=k) for k in (1, 3, 2)]
    barrier(tensor_peers + z_peers + [me.dev(dc=1)])

    rows = pl.ds(pl.multiple_of(piece * 112, 16), 112)
    cp.keep(d.at[rows, columns(me.t, 640)], dd.at[me.t, piece])
    handed = []
    for a, b in ((0, 1), (1, 0), (3, 0), (2, 0), (1, 1), (3, 1), (2, 1)):
        to = me.tensor(dy=a, dx=b)
        handed.append(
            cp.remote(d.at[rows, columns(to, 640)], dd.at[me.t, piece], me.dev(dy=a, dx=b))
        )
    cp.keep(h, hh.at[:, columns(me.t, 896)])

    part = (pl.ds(0, 320), pl.ds(320, 192))
    forward, finish = gather_tensor(
        cp,
        me,
        lambda p: h.at[part[p]],
        lambda t, p: hh.at[part[p], columns(t, 896)],
        part,
    )
    cp.kept[0].wait()
    cp.kept.pop(0)
    for c in handed:
        c.wait_recv()
    over_z = []
    for k in (1, 3, 2):
        over_z.append(cp.remote(dd.at[:, piece], dd.at[:, piece], me.dev(dz=k)))
    side = [cp.remote(dd.at[:, piece], dd.at[:, piece], me.dev(dc=1))]
    forward()
    for k, c in zip((1, 3, 2), over_z):
        c.wait_recv()
        theirs = lax.rem(me.z - k + 4, 4) * 2 + me.core
        side.append(cp.remote(dd.at[:, theirs], dd.at[:, theirs], me.dev(dc=1)))
    finish(nothing)
    for c in side:
        c.wait_recv()
    cp.drain()


def rows_and_weights(s, t, w, p, ss, tt, ww, pp, send, recv, local):
    me = Place()
    cp = Copies(send, recv, local)
    y_peers = [me.dev(dy=k) for k in (1, 3, 2)]
    z_peers = [me.dev(dz=k) for k in (1, 3, 2)]
    sibling = me.dev(dc=1)
    barrier(y_peers + z_peers + [sibling, me.dev(dx=1), me.dev(dh=1)])

    mine = columns(me.core, 256)
    other = columns(1 - me.core, 256)
    cp.keep(w.at[:, mine], ww.at[me.q, me.core])
    cp.keep(p.at[:, mine], pp.at[me.q, me.core])
    swap = [
        cp.remote(w.at[:, other], ww.at[me.q, me.core], sibling),
        cp.remote(p.at[:, other], pp.at[me.q, me.core], sibling),
    ]
    s_part = (pl.ds(0, 32), pl.ds(32, 32))
    t_part = (pl.ds(0, 336), pl.ds(336, 176))
    s_place = lambda b, q: ss.at[me.core, b, s_part[q]]
    t_place = lambda b, q: tt.at[me.core, t_part[q], columns(b, 640)]
    s_forward, s_finish = gather_tensor(cp, me, lambda q: s.at[s_part[q]], s_place, s_part)
    t_forward, t_finish = gather_tensor(cp, me, lambda q: t.at[t_part[q]], t_place, t_part)
    cp.keep(s, ss.at[me.core, me.t])
    cp.keep(t, tt.at[me.core, :, columns(me.t, 640)])

    side = [
        cp.remote(s, ss.at[me.core, me.t], sibling),
        cp.remote(t, tt.at[me.core, :, columns(me.t, 640)], sibling),
    ]
    for c in cp.kept[:2]:
        c.wait()
    del cp.kept[:2]
    for c in swap:
        c.wait_recv()
    over = []
    for ref in (ww, pp):
        over.append(cp.remote(ref.at[me.q], ref.at[me.q], me.dev(dh=1)))
    from_z = []
    for ref in (ww, pp):
        for k in (1, 3, 2):
            from_z.append(cp.remote(ref.at[me.q], ref.at[me.q], me.dev(dz=k)))
    s_forward()
    t_forward()
    far = me.chip(dh=1)
    for ref, c in zip((ww, pp), over):
        c.wait_recv()
        for k in (1, 3, 2):
            from_z.append(cp.remote(ref.at[far], ref.at[far], me.dev(dz=k)))

    def s_side(b):
        block = ss.at[me.core, b]
        side.append(cp.remote(block, block, sibling))

    def t_side(b):
        block = tt.at[me.core, :, columns(b, 640)]
        side.append(cp.remote(block, block, sibling))

    s_finish(s_side)
    t_finish(t_side)
    for c in from_z:
        c.wait_recv()
    for c in side:
        c.wait_recv()
    cp.drain()


def scatter_sums(factor, gw, gp, ow, op, rw, rp, tw, tp, send, recv, local):
    me = Place()
    cp = Copies(send, recv, local)
    offsets = [(a, b) for b in (0, 1) for a in (1, 3, 2, 0) if a or b]
    peers = [me.dev(dz=a, dh=b) for a, b in offsets]
    sibling = me.dev(dc=1)
    barrier(peers + [sibling])
    arrivals = []
    for slot, (a, b) in enumerate(offsets):
        q = me.chip(dz=a, dh=b)
        arrivals.append(cp.remote(gw.at[:, columns(q, 512)], rw.at[slot], me.dev(dz=a, dh=b)))
        arrivals.append(cp.remote(gp.at[:, columns(q, 640)], rp.at[slot], me.dev(dz=a, dh=b)))
    cp.keep(gw.at[:, columns(me.q, 512)], rw.at[7])
    cp.keep(gp.at[:, columns(me.q, 640)], rp.at[7])
    for c in cp.kept:
        c.wait()
    cp.kept.clear()
    for c in arrivals:
        c.wait_recv()

    def add(r, out, tiles):
        for i in range(tiles):
            block = slice(i * 128, i * 128 + 128)
            total = r[7, :, block].astype(F32)
            for slot in range(7):
                total += r[slot, :, block].astype(F32)
            out[block, :] = (total * factor).T

    add(rw, tw, 4)
    add(rp, tp, 5)
    last = []
    mine = columns(me.core, 256)
    for staged, out, rows in ((tw, ow, 256), (tp, op, 320)):
        theirs = pl.ds(pl.multiple_of((1 - me.core) * rows, 64), rows)
        ours = pl.ds(pl.multiple_of(me.core * rows, 64), rows)
        last.append(cp.remote(staged.at[theirs], out.at[:, mine], sibling))
        cp.keep(staged.at[ours], out.at[:, mine])
    for c in last:
        c.wait_recv()
    cp.drain()


ANY = pl.BlockSpec(memory_space=pl.ANY)
VMEM = pl.BlockSpec(memory_space=pltpu.VMEM)


def dma(n):
    return pltpu.SemaphoreType.DMA((n,))


def call(kernel, ident, outs, args, copies, kept, scratch=(), out_spec=ANY):
    return pl.pallas_call(
        kernel,
        out_shape=[jax.ShapeDtypeStruct(shape, dtype) for shape, dtype in outs],
        in_specs=[ANY] * len(args),
        out_specs=[out_spec] * len(outs),
        scratch_shapes=[*scratch, dma(copies), dma(copies), dma(kept)],
        compiler_params=pltpu.CompilerParams(
            collective_id=ident, has_side_effects=True, vmem_limit_bytes=48 * 2**20
        ),
    )(*args)


def dot(a, b, ca, cb):
    return lax.dot_general(a, b, (((ca,), (cb,)), ((), ())), preferred_element_type=F32)


def on_device(teacher_hidden, teacher_down, student_in, student_weight, projection):
    factor = 1.0 / math.sqrt(8192)
    hidden, down = call(
        hidden_and_down,
        1,
        [((512, 7168), BF16), ((8, 8, 112, 640), BF16)],
        (teacher_hidden, teacher_down),
        28,
        2,
    )
    block = dot(hidden, down.reshape(7168, 640), 1, 0).astype(BF16)
    rows, teacher, weight, proj = call(
        rows_and_weights,
        2,
        [((2, 8, 64, 4096), BF16), ((2, 512, 5120), BF16), ((8, 2, 256, 256), BF16), ((8, 2, 320, 256), BF16)],
        (student_in, block, student_weight, projection),
        60,
        4,
    )
    rows = rows.reshape(1024, 4096)
    teacher = teacher.reshape(1024, 5120)
    residual = (
        dot(rows, weight.reshape(4096, 256), 1, 0) - dot(teacher, proj.reshape(5120, 256), 1, 0)
    ).astype(BF16)
    grad_weight = dot(residual, rows, 0, 0).astype(BF16)
    grad_projection = dot(residual, teacher, 0, 0).astype(BF16)
    return call(
        functools.partial(scatter_sums, factor),
        3,
        [((256, 512), F32), ((320, 512), F32)],
        (grad_weight, grad_projection),
        16,
        4,
        (
            pltpu.VMEM((8, 256, 512), BF16),
            pltpu.VMEM((8, 256, 640), BF16),
            pltpu.VMEM((512, 256), F32),
            pltpu.VMEM((640, 256), F32),
        ),
        VMEM,
    )


def solution(mesh):
    in_specs = (
        P("dp", "tensor"),
        P("tensor", None),
        P(("dp", "tensor"), None),
        P("dp", "tensor"),
        P("dp", "tensor"),
    )
    out_specs = (P("dp", "tensor"), P("dp", "tensor"))

    def run(*args):
        return tuple(on_device(*args))

    return jax.shard_map(run, mesh=mesh, in_specs=in_specs, out_specs=out_specs, check_vma=False)
```

time: 777 us -> 265 us (0.34)
  blocking collectives: 509 us -> 0 us
  Pallas kernels: 0 us -> 235 us
  waiting for transfers between devices: 211 us -> 0 us
  matrix products: 38.3 us -> 25.2 us
  between operations: 13.8 us -> 0.8 us
    psum x1 -> x0, blocking collectives: 509 us -> none  [on_device(): teacher_out = lax.psum(partial_value, 'tensor').astype(jnp.bfloat16)]
    pallas_call x0 -> x3, Pallas kernels: none -> 235 us  [call(): pl.pallas_call(kernel, out_shape=[jax.ShapeDtypeStruct(shape, dtype) for...]
    reduce_scatter x2 -> x0, waiting for transfers between devices: 209 us -> none  [on_device(): lax.psum_scatter(contract_rows(inputs, residual), 'dp', scatter_dimension...]
    dot_general x5, matrix products: 38.3 us -> 25.2 us  [dot(): lax.dot_general(a, b, (((ca,), (cb,)), ((), ())), preferred_element_type=...]
  transfers between devices with their start and end apart: 5 -> 0, of which waited for: 2 -> 0; matrix products, arithmetic and copies ran while one was open for 4% -> 0% of each run, Pallas kernels for 0% -> 0%
where the time goes in v1:
time: 265 us
  Pallas kernels  235 us (89%)
  matrix products  25.2 us (10%)
  local copies, waits for them, and re-layouts  4.05 us (2%)
    pallas_call x3, Pallas kernels, call(): pl.pallas_call(kernel, out_shape=[jax.ShapeDtypeStruct(shape, dtype) for...  235 us
    dot_general x5, matrix products, dot(): lax.dot_general(a, b, (((ca,), (cb,)), ((), ())), preferred_element_type=...  25.2 us

profile of v1, /device:TPU:1, one launch (start us, length us, event | category | flops | bytes accessed | tf_op | source)
XLA Modules:
  0.0 264.6 jit_solution(8346554050009503092)
XLA Ops:
  0.6 0.0 copy-start
  0.6 1.2 copy-done
  1.8 84.8 %shard_map.68 = (bf16[512,7168]{1,0:T(8,128)(2,1)}, bf16[8,8,112,640]{3,2,1,0:T(8,128)(2,1)}) custom-call(bf16[512,896]{1,0:T(8,128)(2,1)S(1)} %copy-done, bf16[896,5120]{1,0:T(8,128)(2,1)} %d.1), custom_call_target="tpu_custom_call" | custom-call | tf_op jit(solution)/shard_map/pallas_call | solution.py:288
  86.6 0.0 copy-start.1
  86.6 0.0 copy-start.2
  86.6 0.0 copy-start.3
  86.6 10.9 %convolution_convert_fusion.2.t = bf16[512,640]{1,0:T(8,128)(2,1)S(1)} fusion(bf16[512,7168]{1,0:T(8,128)(2,1)} %get-tuple-element.8, bf16[7168,640]{1,0:T(8,128)(2,1)} %bitcast.22), kind=kOutput, calls=%fused_computation.2 | convolution fusion | flops 4697948160 | bytes 17170432 | tf_op jit(solution)/shard_map/dot_general | solution.py:301
  97.5 0.0 copy-done.1
  97.5 0.0 copy-done.2
  97.5 0.0 copy-done.3
  97.5 89.4 %shard_map.69 = (bf16[2,8,64,4096]{3,2,1,0:T(8,128)(2,1)}, bf16[2,512,5120]{2,1,0:T(8,128)(2,1)}, bf16[8,2,256,256]{3,2,1,0:T(8,128)(2,1)S(1)}, bf16[8,2,320,256]{3,2,1,0:T(8,128)(2,1)}) custom-call(bf16[64,4096]{1,0:T(8,128)(2,1)S(1)} %copy-done.1, bf16[512,640]{1,0:T(8,128)(2,1)S(1)} %convolution_convert_fusion.2.t, bf16[256,512]{1,0:T(8,128)(2,1)S(1)} %copy-done.3, ...), custom_call_target="tpu_custom_call" | custom-call | tf_op jit(solution)/shard_map/pallas_call | solution.py:288
  186.9 0.0 copy-start.4
  186.9 0.0 copy-start.5
  186.9 0.0 slice-start
  186.9 5.9 %fusion.1 = f32[1024,256]{1,0:T(8,128)S(1)} fusion(bf16[1024,4096]{1,0:T(8,128)(2,1)} %bitcast.18, bf16[4096,256]{1,0:T(8,128)(2,1)S(1)} %bitcast.15), kind=kOutput, calls=%fused_computation.5 | convolution fusion | flops 2147483648 | bytes 11534336 | tf_op jit(solution)/shard_map/dot_general | solution.py:301
  192.8 0.5 copy-done.4
  193.3 0.7 copy-done.5
  194.0 2.9 %fusion = bf16[1024,256]{1,0:T(8,128)(2,1)S(1)} fusion(f32[1024,256]{1,0:T(8,128)S(1)} %fusion.1, bf16[1024,5120]{1,0:T(8,128)(2,1)S(1)} %bitcast.16, bf16[5120,256]{1,0:T(8,128)(2,1)S(1)} %bitcast.23), kind=kOutput, calls=%fused_computation.4 | convolution fusion | flops 2684878848 | bytes 14680064 | tf_op jit(solution)/shard_map/dot_general | solution.py:301
  196.9 3.2 %convolution_convert_fusion.gp = bf16[256,5120]{1,0:T(8,128)(2,1)S(1)} fusion(bf16[1024,256]{1,0:T(8,128)(2,1)S(1)} %fusion, bf16[1024,5120]{1,0:T(8,128)(2,1)S(1)} %bitcast.17), kind=kOutput, calls=%fused_computation | convolution fusion | flops 2685665280 | bytes 13631488 | tf_op jit(solution)/shard_map/dot_general | solution.py:301
  200.1 0.0 slice-done
  200.1 2.4 convolution_convert_fusion.1.gw
  202.5 60.5 %shard_map.70 = (f32[256,512]{1,0:T(8,128)S(1)}, f32[320,512]{1,0:T(8,128)S(1)}) custom-call(bf16[256,4096]{1,0:T(8,128)(2,1)S(1)} %convolution_convert_fusion.1.gw, bf16[256,5120]{1,0:T(8,128)(2,1)S(1)} %convolution_convert_fusion.gp), custom_call_target="tpu_custom_call" | custom-call | tf_op jit(solution)/shard_map/pallas_call | solution.py:288
  263.0 0.8 copy.9
  263.8 0.8 copy.10
  (3 shorter events, 0.0 us)
Async XLA Ops:
  0.6 1.2 copy-start
  86.6 10.9 %copy-start.1 = (bf16[64,4096]{1,0:T(8,128)(2,1)S(1)}, bf16[64,4096]{1,0:T(8,128)(2,1)}, u32[]{:S(2)}) copy-start(bf16[64,4096]{1,0:T(8,128)(2,1)} %s.1) | copy-start | bytes 1572868
  86.6 10.9 %copy-start.2 = (bf16[320,512]{1,0:T(8,128)(2,1)S(1)}, bf16[320,512]{1,0:T(8,128)(2,1)}, u32[]{:S(2)}) copy-start(bf16[320,512]{1,0:T(8,128)(2,1)} %p.1) | copy-start | bytes 983044
  86.6 10.9 %copy-start.3 = (bf16[256,512]{1,0:T(8,128)(2,1)S(1)}, bf16[256,512]{1,0:T(8,128)(2,1)}, u32[]{:S(2)}) copy-start(bf16[256,512]{1,0:T(8,128)(2,1)} %w.1) | copy-start | bytes 786436
  186.9 6.4 %copy-start.4 = (bf16[2,512,5120]{2,1,0:T(8,128)(2,1)S(1)}, bf16[2,512,5120]{2,1,0:T(8,128)(2,1)}, u32[]{:S(2)}) copy-start(bf16[2,512,5120]{2,1,0:T(8,128)(2,1)} %get-tuple-element.12) | copy-start | bytes 31457284
  186.9 7.1 %copy-start.5 = (bf16[8,2,320,256]{3,2,1,0:T(8,128)(2,1)S(1)}, bf16[8,2,320,256]{3,2,1,0:T(8,128)(2,1)}, u32[]{:S(2)}) copy-start(bf16[8,2,320,256]{3,2,1,0:T(8,128)(2,1)} %get-tuple-element.13) | copy-start | bytes 7864324
  186.9 13.2 %slice-start = ((s8[8388608]{0:T(1024)(128)(4,1)}), s8[4194304]{0:T(1024)(128)(4,1)S(1)}, s32[]{:S(2)}) async-start(s8[8388608]{0:T(1024)(128)(4,1)} %bitcast.19), calls=%async_computation | async-start | bytes 8388608
  194.0 6.1 %slice-start.1 = ((s8[8388608]{0:T(1024)(128)(4,1)}), s8[4194304]{0:T(1024)(128)(4,1)S(1)}, s32[]{:S(2)}) async-start(s8[8388608]{0:T(1024)(128)(4,1)} %bitcast.19), calls=%async_computation.1 | async-start | bytes 8388608

commit v2 on v1

v2 whole, which is shorter than its diff:
```python
import functools
import math

import jax
import jax.numpy as jnp
from jax import lax
from jax.experimental import pallas as pl
from jax.experimental.pallas import tpu as pltpu
from jax.sharding import PartitionSpec as P

MESH = pl.DeviceIdType.MESH
BF16 = jnp.bfloat16
F32 = jnp.float32


class Place:
    def __init__(self):
        self.d = lax.axis_index("dp")
        self.t = lax.axis_index("tensor")
        self.core = lax.rem(self.d, 2)
        self.q = lax.div(self.d, 2)
        self.z = lax.rem(self.q, 4)
        self.xh = lax.div(self.q, 4)
        self.y = lax.div(self.t, 2)
        self.xl = lax.rem(self.t, 2)

    def dev(self, dy=0, dx=0, dz=0, dh=0, dc=0):
        d = self.dp(dz, dh, dc)
        return (d, self.tensor(dy, dx))

    def tensor(self, dy=0, dx=0):
        return lax.rem(self.y + dy + 4, 4) * 2 + lax.rem(self.xl + dx, 2)

    def chip(self, dz=0, dh=0):
        return lax.rem(self.xh + dh, 2) * 4 + lax.rem(self.z + dz + 4, 4)

    def dp(self, dz=0, dh=0, dc=0):
        return self.chip(dz, dh) * 2 + lax.rem(self.core + dc, 2)


class Copies:
    def __init__(self, send, recv, local):
        self.send, self.recv, self.local = send, recv, local
        self.n = 0
        self.m = 0
        self.sent = []
        self.kept = []

    def remote(self, src, dst, to):
        c = pltpu.make_async_remote_copy(
            src_ref=src,
            dst_ref=dst,
            send_sem=self.send.at[self.n],
            recv_sem=self.recv.at[self.n],
            device_id=to,
            device_id_type=MESH,
        )
        self.n += 1
        c.start()
        self.sent.append(c)
        return c

    def keep(self, src, dst):
        c = pltpu.make_async_copy(src, dst, self.local.at[self.m])
        self.m += 1
        c.start()
        self.kept.append(c)
        return c

    def drain(self):
        for c in self.kept:
            c.wait()
        for c in self.sent:
            c.wait_send()


def barrier(devices):
    sem = pltpu.get_barrier_semaphore()
    for dev in devices:
        pl.semaphore_signal(sem, inc=1, device_id=dev, device_id_type=MESH)
    pl.semaphore_wait(sem, len(devices))


def columns(index, width):
    return pl.ds(pl.multiple_of(index * width, 128), width)


class Ring:
    def __init__(self, cp, to, own, place):
        self.cp, self.to, self.own, self.place = cp, to, own, place

    def start(self):
        send = lambda h, k: self.cp.remote(self.own(h), self.place(0, h), self.to(k))
        self.left0, self.right1 = send(0, 1), send(1, -1)
        self.left1, self.right0 = send(1, 1), send(0, -1)

    def turn(self):
        self.left0.wait_recv()
        self.far0 = self.cp.remote(self.place(-1, 0), self.place(-1, 0), self.to(1))
        self.right1.wait_recv()
        self.far1 = self.cp.remote(self.place(1, 1), self.place(1, 1), self.to(-1))

    def near(self):
        self.left1.wait_recv()
        self.right0.wait_recv()

    def far(self):
        self.far0.wait_recv()
        self.far1.wait_recv()


class Gather:
    def __init__(self, cp, me, own, place, own_part, part):
        self.cp, self.me, self.part, self.own_part = cp, me, part, own_part
        y = lambda k: me.dev(dy=k)
        self.rings = [
            Ring(cp, y, lambda h, p=p: own(p, h), lambda k, h, p=p: place(me.tensor(dy=k), p, h))
            for p in (0, 1)
        ]
        beside = lambda k, h: place(me.tensor(dy=k, dx=1), 0, h)
        self.beside = Ring(cp, y, lambda h: beside(0, h), beside)

    def to_x(self, k, src, p):
        ref = self.part(self.me.tensor(dy=k), p)
        return self.cp.remote(ref if src is None else src, ref, self.me.dev(dx=1))

    def start(self):
        self.x0 = self.to_x(0, self.own_part(0), 0)
        self.rings[1].start()
        self.rings[0].start()
        self.x1 = [self.to_x(0, self.own_part(1), 1)]

    def pass_on(self):
        self.x0.wait_recv()
        self.beside.start()
        self.rings[1].turn()
        self.rings[0].turn()
        self.rings[1].near()
        self.x1 += [self.to_x(k, None, 1) for k in (1, -1)]
        self.beside.turn()
        self.rings[1].far()
        self.x1.append(self.to_x(2, None, 1))

    def finish(self, done):
        me = self.me
        self.rings[0].near()
        done(me.tensor(dy=-1))
        done(me.tensor(dy=1))
        self.rings[0].far()
        done(me.tensor(dy=2))
        self.x1[0].wait_recv()
        done(me.tensor(dx=1))
        self.beside.near()
        self.x1[1].wait_recv()
        self.x1[2].wait_recv()
        done(me.tensor(dy=1, dx=1))
        done(me.tensor(dy=-1, dx=1))
        self.beside.far()
        self.x1[3].wait_recv()
        done(me.tensor(dy=2, dx=1))


def nothing(t):
    return None


def split(starts, lengths):
    return [[pl.ds(a, n), pl.ds(a + n, n)] for a, n in zip(starts, lengths)]


def hidden_and_down(h, d, hh, dd, send, recv, local):
    me = Place()
    cp = Copies(send, recv, local)
    piece = me.z * 2 + me.core
    others = ((0, 1), (1, 0), (3, 0), (2, 0), (1, 1), (3, 1), (2, 1))
    barrier(
        [me.dev(dy=a, dx=b) for a, b in others]
        + [me.dev(dz=1), me.dev(dz=-1), me.dev(dc=1)]
    )

    rows = pl.ds(pl.multiple_of(piece * 112, 16), 112)
    keep = cp.keep(d.at[rows, columns(me.t, 640)], dd.at[me.t, piece])
    handed = []
    for a, b in others:
        to = me.tensor(dy=a, dx=b)
        handed.append(
            cp.remote(d.at[rows, columns(to, 640)], dd.at[me.t, piece], me.dev(dy=a, dx=b))
        )
    cp.keep(h, hh.at[:, columns(me.t, 896)])

    half = split((0, 288), (144, 112))
    part = (pl.ds(0, 288), pl.ds(288, 224))
    gather = Gather(
        cp,
        me,
        lambda p, i: h.at[half[p][i]],
        lambda t, p, i: hh.at[half[p][i], columns(t, 896)],
        lambda p: h.at[part[p]],
        lambda t, p: hh.at[part[p], columns(t, 896)],
    )
    gather.start()
    keep.wait()
    cp.kept.remove(keep)
    for c in handed:
        c.wait_recv()
    there = lambda k: lax.rem(me.z + k + 4, 4) * 2 + me.core
    over = lambda k, i: dd.at[pl.ds(i * 4, 4), there(k)]
    ring = Ring(cp, lambda k: me.dev(dz=k), lambda i: over(0, i), over)
    ring.start()
    side = [cp.remote(dd.at[:, piece], dd.at[:, piece], me.dev(dc=1))]
    gather.pass_on()
    ring.turn()
    ring.near()
    for k in (1, -1):
        side.append(cp.remote(dd.at[:, there(k)], dd.at[:, there(k)], me.dev(dc=1)))
    ring.far()
    side.append(cp.remote(dd.at[:, there(2)], dd.at[:, there(2)], me.dev(dc=1)))
    gather.finish(nothing)
    for c in side:
        c.wait_recv()
    cp.drain()


def rows_and_weights(s, t, w, p, ss, tt, ww, pp, send, recv, local):
    me = Place()
    cp = Copies(send, recv, local)
    sibling = me.dev(dc=1)
    barrier(
        [me.dev(dy=1), me.dev(dy=-1), me.dev(dz=1), me.dev(dz=-1)]
        + [sibling, me.dev(dx=1), me.dev(dh=1)]
    )

    mine = columns(me.core, 256)
    other = columns(1 - me.core, 256)
    weights = ((w, ww), (p, pp))
    keeps = [cp.keep(a.at[:, mine], b.at[me.q, me.core]) for a, b in weights]
    swap = [cp.remote(a.at[:, other], b.at[me.q, me.core], sibling) for a, b in weights]
    s_half = split((0, 2304), (1152, 896))
    s_part = (pl.ds(0, 2304), pl.ds(2304, 1792))
    t_half = split((0, 288), (144, 112))
    t_part = (pl.ds(0, 288), pl.ds(288, 224))
    rows = Gather(
        cp,
        me,
        lambda a, i: s.at[:, s_half[a][i]],
        lambda b, a, i: ss.at[me.core, b, :, s_half[a][i]],
        lambda a: s.at[:, s_part[a]],
        lambda b, a: ss.at[me.core, b, :, s_part[a]],
    )
    teacher = Gather(
        cp,
        me,
        lambda a, i: t.at[t_half[a][i]],
        lambda b, a, i: tt.at[me.core, t_half[a][i], columns(b, 640)],
        lambda a: t.at[t_part[a]],
        lambda b, a: tt.at[me.core, t_part[a], columns(b, 640)],
    )
    rows.start()
    teacher.start()
    cp.keep(s, ss.at[me.core, me.t])
    cp.keep(t, tt.at[me.core, :, columns(me.t, 640)])
    side = [
        cp.remote(s, ss.at[me.core, me.t], sibling),
        cp.remote(t, tt.at[me.core, :, columns(me.t, 640)], sibling),
    ]
    for c in keeps:
        c.wait()
        cp.kept.remove(c)
    for c in swap:
        c.wait_recv()
    over = [cp.remote(b.at[me.q], b.at[me.q], me.dev(dh=1)) for a, b in weights]

    def ring(ref, dh):
        block = lambda k, i: ref.at[me.chip(dz=k, dh=dh), i]
        return Ring(cp, lambda k: me.dev(dz=k), lambda i: block(0, i), block)

    rings = [ring(b, 0) for a, b in weights]
    far = [ring(b, 1) for a, b in weights]
    for r in rings:
        r.start()
    rows.pass_on()
    for c, r in zip(over, far):
        c.wait_recv()
        r.start()
    teacher.pass_on()
    for r in rings + far:
        r.turn()

    def s_side(b):
        block = ss.at[me.core, b]
        side.append(cp.remote(block, block, sibling))

    def t_side(b):
        block = tt.at[me.core, :, columns(b, 640)]
        side.append(cp.remote(block, block, sibling))

    rows.finish(s_side)
    teacher.finish(t_side)
    for r in rings + far:
        r.near()
        r.far()
    for c in side:
        c.wait_recv()
    cp.drain()


def scatter_sums(factor, gw, gp, ow, op, rx, sx, rz, rw, sw, rh, tw, tp, send, recv, local):
    me = Place()
    cp = Copies(send, recv, local)
    across, sibling = me.dev(dh=1), me.dev(dc=1)
    barrier([me.dev(dz=k) for k in (1, 2, 3)] + [across, sibling])
    chunk = lambda g, width, **to: g.at[:, columns(me.chip(**to), width)]
    from_x, from_z = {}, {}
    for k in (2, 1, 3, 0):
        from_x[k] = cp.remote(chunk(gp, 640, dz=k, dh=1), rx.at[k], across)
    for h in (1, 0):
        for k in (2, 1, 3):
            from_z[h, k] = cp.remote(chunk(gw, 512, dz=k, dh=h), rw.at[h, k - 1], me.dev(dz=k))

    def total(mine, base, others, tile):
        out = mine[:, columns(base + tile, 128)].astype(F32)
        for r in others:
            out += r[:, tile * 128 : tile * 128 + 128].astype(F32)
        return out

    second = {}
    for k in (2, 1, 3):
        from_x[k].wait_recv()
        for i in range(5):
            sx[k - 1, :, i * 128 : i * 128 + 128] = total(
                gp, me.chip(dz=k) * 5, [rx.at[k]], i
            ).astype(BF16)
        second[k] = cp.remote(sx.at[k - 1], rz.at[k - 1], me.dev(dz=k))
    for k in (2, 1, 3):
        from_z[1, k].wait_recv()
    for i in range(4):
        sw[:, i * 128 : i * 128 + 128] = total(
            gw, me.chip(dh=1) * 4, [rw.at[1, k] for k in range(3)], i
        ).astype(BF16)
    back = cp.remote(sw, rh, across)

    mine = columns(me.core, 256)
    last = []

    def hand_out(g, staged, out, rows, others):
        tiles = rows // 64
        for i in range(tiles):
            value = total(g, me.q * tiles, others, i) * factor
            staged[i * 128 : i * 128 + 128, :] = value.T
        theirs = pl.ds(pl.multiple_of((1 - me.core) * rows, 64), rows)
        ours = pl.ds(pl.multiple_of(me.core * rows, 64), rows)
        last.append(cp.remote(staged.at[theirs], out.at[:, mine], sibling))
        cp.keep(staged.at[ours], out.at[:, mine])

    from_x[0].wait_recv()
    for k in (2, 1, 3):
        second[k].wait_recv()
    hand_out(gp, tp, op, 320, [rx.at[0]] + [rz.at[k] for k in range(3)])
    for k in (2, 1, 3):
        from_z[0, k].wait_recv()
    back.wait_recv()
    hand_out(gw, tw, ow, 256, [rw.at[0, k] for k in range(3)] + [rh])
    for c in last:
        c.wait_recv()
    cp.drain()


ANY = pl.BlockSpec(memory_space=pl.ANY)
VMEM = pl.BlockSpec(memory_space=pltpu.VMEM)


def dma(n):
    return pltpu.SemaphoreType.DMA((n,))


def call(kernel, ident, outs, args, copies, kept, scratch=(), spec=ANY):
    return pl.pallas_call(
        kernel,
        out_shape=[jax.ShapeDtypeStruct(shape, dtype) for shape, dtype in outs],
        in_specs=[spec] * len(args),
        out_specs=[spec] * len(outs),
        scratch_shapes=[*scratch, dma(copies), dma(copies), dma(kept)],
        compiler_params=pltpu.CompilerParams(
            collective_id=ident, has_side_effects=True, vmem_limit_bytes=48 * 2**20
        ),
    )(*args)


def dot(a, b, ca, cb):
    return lax.dot_general(a, b, (((ca,), (cb,)), ((), ())), preferred_element_type=F32)


def on_device(teacher_hidden, teacher_down, student_in, student_weight, projection):
    factor = 1.0 / math.sqrt(8192)
    hidden, down = call(
        hidden_and_down,
        1,
        [((512, 7168), BF16), ((8, 8, 112, 640), BF16)],
        (teacher_hidden, teacher_down),
        48,
        2,
    )
    block = dot(hidden, down.reshape(7168, 640), 1, 0).astype(BF16)
    rows, teacher, weight, proj = call(
        rows_and_weights,
        2,
        [((2, 8, 64, 4096), BF16), ((2, 512, 5120), BF16), ((8, 2, 256, 256), BF16), ((8, 2, 320, 256), BF16)],
        (student_in, block, student_weight, projection),
        96,
        4,
    )
    rows = rows.reshape(1024, 4096)
    teacher = teacher.reshape(1024, 5120)
    residual = (
        dot(rows, weight.reshape(4096, 256), 1, 0) - dot(teacher, proj.reshape(5120, 256), 1, 0)
    ).astype(BF16)
    grad_weight = dot(residual, rows, 0, 0).astype(BF16)
    grad_projection = dot(residual, teacher, 0, 0).astype(BF16)
    vmem = lambda *shape: pltpu.VMEM(shape, BF16)
    return call(
        functools.partial(scatter_sums, factor),
        3,
        [((256, 512), F32), ((320, 512), F32)],
        (grad_weight, grad_projection),
        16,
        2,
        (
            vmem(4, 256, 640),
            vmem(3, 256, 640),
            vmem(3, 256, 640),
            vmem(2, 3, 256, 512),
            vmem(256, 512),
            vmem(256, 512),
            pltpu.VMEM((512, 256), F32),
            pltpu.VMEM((640, 256), F32),
        ),
        VMEM,
    )


def solution(mesh):
    in_specs = (
        P("dp", "tensor"),
        P("tensor", None),
        P(("dp", "tensor"), None),
        P("dp", "tensor"),
        P("dp", "tensor"),
    )
    out_specs = (P("dp", "tensor"), P("dp", "tensor"))

    def run(*args):
        return tuple(on_device(*args))

    return jax.shard_map(run, mesh=mesh, in_specs=in_specs, out_specs=out_specs, check_vma=False)
```

time: 265 us -> 228 us (0.86)
  Pallas kernels: 235 us -> 198 us
    pallas_call x3, Pallas kernels: 235 us -> 198 us  [call(): pl.pallas_call(kernel, out_shape=[jax.ShapeDtypeStruct(shape, dtype) for...]
where the time goes in v2:
time: 228 us
  Pallas kernels  198 us (87%)
  matrix products  25.4 us (11%)
  local copies, waits for them, and re-layouts  4.04 us (2%)
    pallas_call x3, Pallas kernels, call(): pl.pallas_call(kernel, out_shape=[jax.ShapeDtypeStruct(shape, dtype) for...  198 us
    dot_general x5, matrix products, dot(): lax.dot_general(a, b, (((ca,), (cb,)), ((), ())), preferred_element_type=...  25.4 us

profile of v2, /device:TPU:1, one launch (start us, length us, event | category | flops | bytes accessed | tf_op | source)
XLA Modules:
  0.0 227.9 jit_solution(11909757493921851706)
XLA Ops:
  0.6 0.0 copy-start
  0.6 1.2 copy-done
  1.8 74.7 %shard_map.68 = (bf16[512,7168]{1,0:T(8,128)(2,1)}, bf16[8,8,112,640]{3,2,1,0:T(8,128)(2,1)}) custom-call(bf16[512,896]{1,0:T(8,128)(2,1)S(1)} %copy-done, bf16[896,5120]{1,0:T(8,128)(2,1)} %d.1), custom_call_target="tpu_custom_call" | custom-call | tf_op jit(solution)/shard_map/pallas_call | solution.py:377
  76.6 0.0 copy-start.1
  76.6 0.0 copy-start.2
  76.6 0.0 copy-start.3
  76.6 10.9 %convolution_convert_fusion.2.t = bf16[512,640]{1,0:T(8,128)(2,1)S(1)} fusion(bf16[512,7168]{1,0:T(8,128)(2,1)} %get-tuple-element.8, bf16[7168,640]{1,0:T(8,128)(2,1)} %bitcast.22), kind=kOutput, calls=%fused_computation.2 | convolution fusion | flops 4697948160 | bytes 17170432 | tf_op jit(solution)/shard_map/dot_general | solution.py:390
  87.5 0.0 copy-done.1
  87.5 0.0 copy-done.2
  87.5 0.0 copy-done.3
  87.5 79.3 %shard_map.69 = (bf16[2,8,64,4096]{3,2,1,0:T(8,128)(2,1)}, bf16[2,512,5120]{2,1,0:T(8,128)(2,1)}, bf16[8,2,256,256]{3,2,1,0:T(8,128)(2,1)S(1)}, bf16[8,2,320,256]{3,2,1,0:T(8,128)(2,1)}) custom-call(bf16[64,4096]{1,0:T(8,128)(2,1)S(1)} %copy-done.1, bf16[512,640]{1,0:T(8,128)(2,1)S(1)} %convolution_convert_fusion.2.t, bf16[256,512]{1,0:T(8,128)(2,1)S(1)} %copy-done.3, ...), custom_call_target="tpu_custom_call" | custom-call | tf_op jit(solution)/shard_map/pallas_call | solution.py:377
  166.8 0.0 copy-start.4
  166.8 0.0 copy-start.5
  166.8 0.0 slice-start
  166.8 5.9 %fusion.1 = f32[1024,256]{1,0:T(8,128)S(1)} fusion(bf16[1024,4096]{1,0:T(8,128)(2,1)} %bitcast.18, bf16[4096,256]{1,0:T(8,128)(2,1)S(1)} %bitcast.15), kind=kOutput, calls=%fused_computation.5 | convolution fusion | flops 2147483648 | bytes 11534336 | tf_op jit(solution)/shard_map/dot_general | solution.py:390
  172.7 0.5 copy-done.4
  173.1 0.7 copy-done.5
  173.9 2.9 %fusion = bf16[1024,256]{1,0:T(8,128)(2,1)S(1)} fusion(f32[1024,256]{1,0:T(8,128)S(1)} %fusion.1, bf16[1024,5120]{1,0:T(8,128)(2,1)S(1)} %bitcast.16, bf16[5120,256]{1,0:T(8,128)(2,1)S(1)} %bitcast.23), kind=kOutput, calls=%fused_computation.4 | convolution fusion | flops 2684878848 | bytes 14680064 | tf_op jit(solution)/shard_map/dot_general | solution.py:390
  176.8 3.4 %convolution_convert_fusion.gp = bf16[256,5120]{1,0:T(8,128)(2,1)S(1)} fusion(bf16[1024,256]{1,0:T(8,128)(2,1)S(1)} %fusion, bf16[1024,5120]{1,0:T(8,128)(2,1)S(1)} %bitcast.17), kind=kOutput, calls=%fused_computation | convolution fusion | flops 2685665280 | bytes 13631488 | tf_op jit(solution)/shard_map/dot_general | solution.py:390
  180.1 0.0 slice-done
  180.2 2.4 %convolution_convert_fusion.1.gw = bf16[256,4096]{1,0:T(8,128)(2,1)S(1)} fusion(bf16[1024,256]{1,0:T(8,128)(2,1)S(1)} %fusion, bf16[1024,4096]{1,0:T(8,128)(2,1)S(1)} %bitcast.21), kind=kOutput, calls=%fused_computation.1 | convolution fusion | flops 2148532224 | bytes 11010048 | tf_op jit(solution)/shard_map/dot_general | solution.py:390
  182.6 43.7 %shard_map.70 = (f32[256,512]{1,0:T(8,128)S(1)}, f32[320,512]{1,0:T(8,128)S(1)}) custom-call(bf16[256,4096]{1,0:T(8,128)(2,1)S(1)} %convolution_convert_fusion.1.gw, bf16[256,5120]{1,0:T(8,128)(2,1)S(1)} %convolution_convert_fusion.gp), custom_call_target="tpu_custom_call" | custom-call | tf_op jit(solution)/shard_map/pallas_call | solution.py:377
  226.2 0.8 copy.9
  227.0 0.8 copy.10
  (3 shorter events, 0.0 us)
Async XLA Ops:
  0.6 1.2 copy-start
  76.6 10.9 %copy-start.1 = (bf16[64,4096]{1,0:T(8,128)(2,1)S(1)}, bf16[64,4096]{1,0:T(8,128)(2,1)}, u32[]{:S(2)}) copy-start(bf16[64,4096]{1,0:T(8,128)(2,1)} %s.1) | copy-start | bytes 1572868
  76.6 10.9 %copy-start.2 = (bf16[320,512]{1,0:T(8,128)(2,1)S(1)}, bf16[320,512]{1,0:T(8,128)(2,1)}, u32[]{:S(2)}) copy-start(bf16[320,512]{1,0:T(8,128)(2,1)} %p.1) | copy-start | bytes 983044
  76.6 10.9 %copy-start.3 = (bf16[256,512]{1,0:T(8,128)(2,1)S(1)}, bf16[256,512]{1,0:T(8,128)(2,1)}, u32[]{:S(2)}) copy-start(bf16[256,512]{1,0:T(8,128)(2,1)} %w.1) | copy-start | bytes 786436
  166.8 6.4 %copy-start.4 = (bf16[2,512,5120]{2,1,0:T(8,128)(2,1)S(1)}, bf16[2,512,5120]{2,1,0:T(8,128)(2,1)}, u32[]{:S(2)}) copy-start(bf16[2,512,5120]{2,1,0:T(8,128)(2,1)} %get-tuple-element.12) | copy-start | bytes 31457284
  166.8 7.1 %copy-start.5 = (bf16[8,2,320,256]{3,2,1,0:T(8,128)(2,1)S(1)}, bf16[8,2,320,256]{3,2,1,0:T(8,128)(2,1)}, u32[]{:S(2)}) copy-start(bf16[8,2,320,256]{3,2,1,0:T(8,128)(2,1)} %get-tuple-element.13) | copy-start | bytes 7864324
  166.8 13.4 %slice-start = ((s8[8388608]{0:T(1024)(128)(4,1)}), s8[4194304]{0:T(1024)(128)(4,1)S(1)}, s32[]{:S(2)}) async-start(s8[8388608]{0:T(1024)(128)(4,1)} %bitcast.19), calls=%async_computation | async-start | bytes 8388608
  173.9 6.3 %slice-start.1 = ((s8[8388608]{0:T(1024)(128)(4,1)}), s8[4194304]{0:T(1024)(128)(4,1)S(1)}, s32[]{:S(2)}) async-start(s8[8388608]{0:T(1024)(128)(4,1)} %bitcast.19), calls=%async_computation.1 | async-start | bytes 8388608

commit v3 on v2

v3 whole, which is shorter than its diff:
```python
import functools
import math

import jax
import jax.numpy as jnp
from jax import lax
from jax.experimental import pallas as pl
from jax.experimental.pallas import tpu as pltpu
from jax.sharding import PartitionSpec as P

MESH = pl.DeviceIdType.MESH
BF16 = jnp.bfloat16
F32 = jnp.float32
COPIES = 152


class Place:
    def __init__(self):
        self.d = lax.axis_index("dp")
        self.t = lax.axis_index("tensor")
        self.core = lax.rem(self.d, 2)
        self.q = lax.div(self.d, 2)
        self.z = lax.rem(self.q, 4)
        self.xh = lax.div(self.q, 4)
        self.y = lax.div(self.t, 2)
        self.xl = lax.rem(self.t, 2)

    def dev(self, dy=0, dx=0, dz=0, dh=0, dc=0):
        d = self.dp(dz, dh, dc)
        return (d, self.tensor(dy, dx))

    def tensor(self, dy=0, dx=0):
        return lax.rem(self.y + dy + 4, 4) * 2 + lax.rem(self.xl + dx, 2)

    def chip(self, dz=0, dh=0):
        return lax.rem(self.xh + dh, 2) * 4 + lax.rem(self.z + dz + 4, 4)

    def dp(self, dz=0, dh=0, dc=0):
        return self.chip(dz, dh) * 2 + lax.rem(self.core + dc, 2)


class Copies:
    def __init__(self, send, recv, local):
        self.send, self.recv, self.local = send, recv, local
        self.n = 0
        self.m = 0
        self.sent = []
        self.kept = []

    def remote(self, src, dst, to):
        c = pltpu.make_async_remote_copy(
            src_ref=src,
            dst_ref=dst,
            send_sem=self.send.at[self.n],
            recv_sem=self.recv.at[self.n],
            device_id=to,
            device_id_type=MESH,
        )
        self.n += 1
        c.start()
        self.sent.append(c)
        return c

    def keep(self, src, dst):
        c = pltpu.make_async_copy(src, dst, self.local.at[self.m])
        self.m += 1
        c.start()
        self.kept.append(c)
        return c

    def kept_now(self, c):
        c.wait()
        self.kept = [k for k in self.kept if k is not c]

    def drain(self):
        for c in self.kept:
            c.wait()
        for c in self.sent:
            c.wait_send()


def barrier(devices):
    sem = pltpu.get_barrier_semaphore()
    for dev in devices:
        pl.semaphore_signal(sem, inc=1, device_id=dev, device_id_type=MESH)
    pl.semaphore_wait(sem, len(devices))


def columns(index, width):
    return pl.ds(pl.multiple_of(index * width, 128), width)


class Ring:
    def __init__(self, cp, to, own, place):
        self.cp, self.to, self.own, self.place = cp, to, own, place

    def start(self):
        send = lambda h, k: self.cp.remote(self.own(h), self.place(0, h), self.to(k))
        self.left0, self.right1 = send(0, 1), send(1, -1)
        self.left1, self.right0 = send(1, 1), send(0, -1)

    def turn(self):
        self.left0.wait_recv()
        self.far0 = self.cp.remote(self.place(-1, 0), self.place(-1, 0), self.to(1))
        self.right1.wait_recv()
        self.far1 = self.cp.remote(self.place(1, 1), self.place(1, 1), self.to(-1))

    def near(self):
        self.left1.wait_recv()
        self.right0.wait_recv()

    def far(self):
        self.far0.wait_recv()
        self.far1.wait_recv()


class Gather:
    def __init__(self, cp, me, own, place, own_part, part):
        self.cp, self.me, self.part, self.own_part = cp, me, part, own_part
        y = lambda k: me.dev(dy=k)
        self.rings = [
            Ring(cp, y, lambda h, p=p: own(p, h), lambda k, h, p=p: place(me.tensor(dy=k), p, h))
            for p in (0, 1)
        ]
        beside = lambda k, h: place(me.tensor(dy=k, dx=1), 0, h)
        self.beside = Ring(cp, y, lambda h: beside(0, h), beside)

    def to_x(self, k, src, p):
        ref = self.part(self.me.tensor(dy=k), p)
        return self.cp.remote(ref if src is None else src, ref, self.me.dev(dx=1))

    def start(self):
        self.x0 = self.to_x(0, self.own_part(0), 0)
        self.rings[1].start()
        self.rings[0].start()
        self.x1 = [self.to_x(0, self.own_part(1), 1)]

    def pass_on(self):
        self.x0.wait_recv()
        self.beside.start()
        self.rings[1].turn()
        self.rings[0].turn()
        self.rings[1].near()
        self.x1 += [self.to_x(k, None, 1) for k in (1, -1)]
        self.beside.turn()
        self.rings[1].far()
        self.x1.append(self.to_x(2, None, 1))

    def finish(self, done):
        me = self.me
        self.rings[0].near()
        done(me.tensor(dy=-1))
        done(me.tensor(dy=1))
        self.rings[0].far()
        done(me.tensor(dy=2))

    def finish_beside(self, done):
        me = self.me
        self.x1[0].wait_recv()
        done(me.tensor(dx=1))
        self.beside.near()
        self.x1[1].wait_recv()
        self.x1[2].wait_recv()
        done(me.tensor(dy=1, dx=1))
        done(me.tensor(dy=-1, dx=1))
        self.beside.far()
        self.x1[3].wait_recv()
        done(me.tensor(dy=2, dx=1))


def nothing(t):
    return None


def split(starts, lengths):
    return [[pl.ds(a, n), pl.ds(a + n, n)] for a, n in zip(starts, lengths)]


def dot(a, b):
    return jnp.dot(a, b, preferred_element_type=F32)


def distill(
    factor,
    h, d, s, w, p,
    ow, op,
    hh, dd, ss, tt, ww, pp, tacc, racc, rest,
    gx, gp, gw, rx, sx, rz, rw, sw, rh, tw, tp,
    send, recv, local,
):
    me = Place()
    cp = Copies(send, recv, local)
    sibling, across = me.dev(dc=1), me.dev(dh=1)
    others = ((0, 1), (1, 0), (3, 0), (2, 0), (1, 1), (3, 1), (2, 1))
    barrier(
        [me.dev(dy=a, dx=b) for a, b in others]
        + [me.dev(dz=k) for k in (1, 3, 2)]
        + [sibling, across]
    )

    piece = me.z * 2 + me.core
    rows = pl.ds(pl.multiple_of(piece * 112, 16), 112)
    first = [cp.keep(d.at[rows, columns(me.t, 640)], dd.at[me.t, piece])]
    handed = []
    for a, b in others:
        to = me.tensor(dy=a, dx=b)
        handed.append(
            cp.remote(d.at[rows, columns(to, 640)], dd.at[me.t, piece], me.dev(dy=a, dx=b))
        )
    hidden_keep = cp.keep(h, hh.at[:, columns(me.t, 896)])
    half = split((0, 288), (144, 112))
    part = (pl.ds(0, 288), pl.ds(288, 224))
    hidden = Gather(
        cp,
        me,
        lambda p, i: h.at[half[p][i]],
        lambda t, p, i: hh.at[half[p][i], columns(t, 896)],
        lambda p: h.at[part[p]],
        lambda t, p: hh.at[part[p], columns(t, 896)],
    )
    hidden.start()

    mine, other = columns(me.core, 256), columns(1 - me.core, 256)
    weights = ((w, ww, 256), (p, pp, 320))
    at = lambda q, c, n: pl.ds(pl.multiple_of((q * 2 + c) * n, 64), n)
    pair = lambda q, n: pl.ds(pl.multiple_of(q * 2 * n, 128), 2 * n)
    first += [cp.keep(a.at[:, mine], b.at[at(me.q, me.core, n)]) for a, b, n in weights]
    swap = [
        cp.remote(a.at[:, other], b.at[at(me.q, me.core, n)], sibling) for a, b, n in weights
    ]

    for c in first:
        cp.kept_now(c)
    for c in handed:
        c.wait_recv()
    there = lambda k: lax.rem(me.z + k + 4, 4) * 2 + me.core
    over = lambda k, i: dd.at[pl.ds(i * 4, 4), there(k)]
    down = Ring(cp, lambda k: me.dev(dz=k), lambda i: over(0, i), over)
    down.start()
    down_side = []

    def pass_down(k):
        block = dd.at[:, there(k)]
        down_side.append(cp.remote(block, block, sibling))

    pass_down(0)
    hidden.pass_on()

    s_half = split((0, 2304), (1152, 896))
    s_part = (pl.ds(0, 2304), pl.ds(2304, 1792))
    s_rows = lambda b: pl.ds(pl.multiple_of((me.core * 8 + b) * 64, 64), 64)
    student = Gather(
        cp,
        me,
        lambda a, i: s.at[:, s_half[a][i]],
        lambda b, a, i: ss.at[s_rows(b), s_half[a][i]],
        lambda a: s.at[:, s_part[a]],
        lambda b, a: ss.at[s_rows(b), s_part[a]],
    )
    student.start()
    student_keep = cp.keep(s, ss.at[s_rows(me.t)])
    student_side = [cp.remote(s, ss.at[s_rows(me.t)], sibling)]
    for c in swap:
        c.wait_recv()
    far_weights = [
        cp.remote(b.at[pair(me.q, n)], b.at[pair(me.q, n)], across) for a, b, n in weights
    ]
    down.turn()
    down.near()
    pass_down(1)
    pass_down(-1)

    def ring(ref, n, dh):
        block = lambda k, i: ref.at[at(me.chip(dz=k, dh=dh), i, n)]
        return Ring(cp, lambda k: me.dev(dz=k), lambda i: block(0, i), block)

    near_rings = [ring(b, n, 0) for a, b, n in weights]
    far_rings = [ring(b, n, 1) for a, b, n in weights]
    for r in near_rings:
        r.start()
    down.far()
    pass_down(2)

    tacc[...] = jnp.zeros_like(tacc)

    def teacher_blocks(dx):
        @pl.loop(0, 4)
        def _(k):
            b = me.tensor(dy=k, dx=dx)
            left = hh[:, columns(b, 896)]
            right = dd.at[b]
            for n in (slice(0, 256), slice(256, 512), slice(512, 640)):
                tacc[:, n] += dot(left, right[:, :, n].reshape(896, n.stop - n.start))

    cp.kept_now(hidden_keep)
    hidden.finish(nothing)
    for c in down_side:
        c.wait_recv()
    teacher_blocks(0)
    hidden.finish_beside(nothing)
    teacher_blocks(1)
    half_rows = lambda c: pl.multiple_of(c * 512, 512)
    own_rows = half_rows(me.core)
    own_block = tt.at[pl.ds(own_rows, 512), columns(me.t, 640)]
    own_block[...] = tacc[...].astype(BF16)

    def t_rows(r):
        return pl.ds(pl.multiple_of(own_rows + r.start, 16), r.size)

    teacher = Gather(
        cp,
        me,
        lambda a, i: tt.at[t_rows(half[a][i]), columns(me.t, 640)],
        lambda b, a, i: tt.at[t_rows(half[a][i]), columns(b, 640)],
        lambda a: tt.at[t_rows(part[a]), columns(me.t, 640)],
        lambda b, a: tt.at[t_rows(part[a]), columns(b, 640)],
    )
    teacher.start()
    teacher_side = [cp.remote(own_block, own_block, sibling)]
    student.pass_on()
    for c, r in zip(far_weights, far_rings):
        c.wait_recv()
        r.start()
    for r in near_rings + far_rings:
        r.turn()

    def pass_student(b):
        block = ss.at[s_rows(b)]
        student_side.append(cp.remote(block, block, sibling))

    student.finish(pass_student)
    teacher.pass_on()
    student.finish_beside(pass_student)
    for r in near_rings + far_rings:
        r.near()
        r.far()
    cp.kept_now(student_keep)
    for c in student_side:
        c.wait_recv()

    racc[...] = jnp.zeros_like(racc)

    @pl.loop(0, 8)
    def _(k):
        depth = pl.ds(pl.multiple_of(k * 512, 512), 512)
        racc[...] += dot(ss[:, depth], ww[depth, :])

    def target(core, b):
        at_rows = pl.ds(half_rows(core), 512)
        weight = pp[pl.ds(pl.multiple_of(b * 640, 128), 640), :]
        racc[at_rows, :] -= dot(tt[at_rows, columns(b, 640)], weight)

    order = [me.t]
    target(me.core, me.t)

    def pass_teacher(b):
        block = tt.at[pl.ds(own_rows, 512), columns(b, 640)]
        teacher_side.append(cp.remote(block, block, sibling))
        order.append(b)
        target(me.core, b)
        teacher_side[len(order) - 2].wait_recv()
        target(1 - me.core, order[-2])

    teacher.finish(pass_teacher)
    teacher.finish_beside(pass_teacher)
    teacher_side[-1].wait_recv()
    target(1 - me.core, order[-1])
    for i in range(8):
        block = slice(i * 128, i * 128 + 128)
        rest[:, block] = racc[block, :].T.astype(BF16)

    def project(**to):
        return dot(rest[...], tt[:, columns(me.chip(**to), 640)])

    def weigh(**to):
        return dot(rest[...], ss[:, columns(me.chip(**to), 512)])

    from_x, from_z = {}, {}
    for k in (2, 1, 3, 0):
        gx[k] = project(dz=k, dh=1).astype(BF16)
        from_x[k] = cp.remote(gx.at[k], rx.at[k], across)
    for g in (1, 0):
        for k in (2, 1, 3):
            gw[g, k] = weigh(dz=k, dh=g).astype(BF16)
            from_z[g, k] = cp.remote(gw.at[g, k], rw.at[g, k - 1], me.dev(dz=k))
    second = {}
    for k in (2, 1, 3):
        gp[...] = project(dz=k)
        from_x[k].wait_recv()
        sx[k - 1] = (gp[...] + rx[k].astype(F32)).astype(BF16)
        second[k] = cp.remote(sx.at[k - 1], rz.at[k - 1], me.dev(dz=k))
    gp[:, :512] = weigh(dh=1)
    for k in (2, 1, 3):
        from_z[1, k].wait_recv()
    sw[...] = (
        gp[:, :512] + rw[1, 0].astype(F32) + rw[1, 1].astype(F32) + rw[1, 2].astype(F32)
    ).astype(BF16)
    back = cp.remote(sw, rh, across)
    last = []

    def hand_out(staged, out, n, parts):
        for i in range(n // 64):
            block = slice(i * 128, i * 128 + 128)
            value = gp[:, block]
            for r in parts:
                value += r[:, block].astype(F32)
            staged[block, :] = (value * factor).T
        theirs = pl.ds(pl.multiple_of((1 - me.core) * n, 64), n)
        ours = pl.ds(pl.multiple_of(me.core * n, 64), n)
        last.append(cp.remote(staged.at[theirs], out.at[:, mine], sibling))
        cp.keep(staged.at[ours], out.at[:, mine])

    gp[...] = project()
    from_x[0].wait_recv()
    for k in (2, 1, 3):
        second[k].wait_recv()
    hand_out(tp, op, 320, [rx.at[0]] + [rz.at[k] for k in range(3)])
    gp[:, :512] = weigh()
    for k in (2, 1, 3):
        from_z[0, k].wait_recv()
    back.wait_recv()
    hand_out(tw, ow, 256, [rw.at[0, k] for k in range(3)] + [rh])
    for c in last:
        c.wait_recv()
    cp.drain()


def on_device(*args):
    narrow = lambda *shape: pltpu.VMEM(shape, BF16)
    wide = lambda *shape: pltpu.VMEM(shape, F32)
    return tuple(
        pl.pallas_call(
            functools.partial(distill, 1.0 / math.sqrt(8192)),
            out_shape=[
                jax.ShapeDtypeStruct((256, 512), F32),
                jax.ShapeDtypeStruct((320, 512), F32),
            ],
            in_specs=[pl.BlockSpec(memory_space=pl.ANY)] * 5,
            out_specs=[pl.BlockSpec(memory_space=pltpu.VMEM)] * 2,
            scratch_shapes=[
                narrow(512, 7168),
                narrow(8, 8, 112, 640),
                narrow(1024, 4096),
                narrow(1024, 5120),
                narrow(4096, 256),
                narrow(5120, 256),
                wide(512, 640),
                wide(1024, 256),
                narrow(256, 1024),
                narrow(4, 256, 640),
                wide(256, 640),
                narrow(2, 4, 256, 512),
                narrow(4, 256, 640),
                narrow(3, 256, 640),
                narrow(3, 256, 640),
                narrow(2, 3, 256, 512),
                narrow(256, 512),
                narrow(256, 512),
                wide(512, 256),
                wide(640, 256),
                pltpu.SemaphoreType.DMA((COPIES,)),
                pltpu.SemaphoreType.DMA((COPIES,)),
                pltpu.SemaphoreType.DMA((8,)),
            ],
            compiler_params=pltpu.CompilerParams(
                collective_id=1, has_side_effects=True, vmem_limit_bytes=62 * 2**20
            ),
        )(*args)
    )


def solution(mesh):
    in_specs = (
        P("dp", "tensor"),
        P("tensor", None),
        P(("dp", "tensor"), None),
        P("dp", "tensor"),
        P("dp", "tensor"),
    )
    out_specs = (P("dp", "tensor"), P("dp", "tensor"))

    return jax.shard_map(
        on_device, mesh=mesh, in_specs=in_specs, out_specs=out_specs, check_vma=False
    )
```

time: 228 us -> 202 us (0.89)
  matrix products: 25.4 us -> 0 us
    dot_general x5 -> x0, matrix products: 25.4 us -> none  [dot(): lax.dot_general(a, b, (((ca,), (cb,)), ((), ())), preferred_element_type=...]
    pallas_call x3 -> x1, Pallas kernels: 198 us -> 198 us  [on_device(): pl.pallas_call(functools.partial(distill, 1.0 / math.sqrt(8192)), out_sha...]
where the time goes in v3:
time: 202 us
  Pallas kernels  198 us (98%)
  local copies, waits for them, and re-layouts  3.84 us (2%)
    pallas_call x1, Pallas kernels, on_device(): pl.pallas_call(functools.partial(distill, 1.0 / math.sqrt(8192)), out_sha...  198 us

profile of v3, /device:TPU:1, one launch (start us, length us, event | category | flops | bytes accessed | tf_op | source)
XLA Modules:
  0.0 202.0 jit_solution(14075167817669605367)
XLA Ops:
  0.6 197.6 %shard_map.68 = (f32[256,512]{1,0:T(8,128)}, f32[320,512]{1,0:T(8,128)}) custom-call(bf16[512,896]{1,0:T(8,128)(2,1)} %h.1, bf16[896,5120]{1,0:T(8,128)(2,1)} %d.1, bf16[64,4096]{1,0:T(8,128)(2,1)} %s.1, bf16[256,512]{1,0:T(8,128)(2,1)} %w.1, bf16[320,512]{1,0:T(8,128)(2,1)} %p.1), custom_call_target="tpu_custom_call" | custom-call | tf_op jit(solution)/shard_map/pallas_call | solution.py:432
  198.2 1.9 copy.9
  200.1 2.0 copy.10

commit v4 on v3

v4 whole, which is shorter than its diff:
```python
import functools
import math

import jax
import jax.numpy as jnp
from jax import lax
from jax.experimental import pallas as pl
from jax.experimental.pallas import tpu as pltpu
from jax.sharding import PartitionSpec as P

MESH = pl.DeviceIdType.MESH
BF16 = jnp.bfloat16
F32 = jnp.float32
COPIES = 208
STEPS = 4
VMEM_MIB = 56
STEP = 512 // STEPS


class Place:
    def __init__(self):
        self.d = lax.axis_index("dp")
        self.t = lax.axis_index("tensor")
        self.core = lax.rem(self.d, 2)
        self.q = lax.div(self.d, 2)
        self.z = lax.rem(self.q, 4)
        self.xh = lax.div(self.q, 4)
        self.y = lax.div(self.t, 2)
        self.xl = lax.rem(self.t, 2)

    def dev(self, dy=0, dx=0, dz=0, dh=0, dc=0):
        d = self.dp(dz, dh, dc)
        return (d, self.tensor(dy, dx))

    def tensor(self, dy=0, dx=0):
        return lax.rem(self.y + dy + 4, 4) * 2 + lax.rem(self.xl + dx, 2)

    def chip(self, dz=0, dh=0):
        return lax.rem(self.xh + dh, 2) * 4 + lax.rem(self.z + dz + 4, 4)

    def dp(self, dz=0, dh=0, dc=0):
        return self.chip(dz, dh) * 2 + lax.rem(self.core + dc, 2)


class Copies:
    def __init__(self, send, recv, local):
        self.send, self.recv, self.local = send, recv, local
        self.n = 0
        self.m = 0
        self.sent = []
        self.kept = []

    def remote(self, src, dst, to):
        c = pltpu.make_async_remote_copy(
            src_ref=src,
            dst_ref=dst,
            send_sem=self.send.at[self.n],
            recv_sem=self.recv.at[self.n],
            device_id=to,
            device_id_type=MESH,
        )
        self.n += 1
        c.start()
        self.sent.append(c)
        return c

    def keep(self, src, dst):
        c = pltpu.make_async_copy(src, dst, self.local.at[self.m])
        self.m += 1
        c.start()
        self.kept.append(c)
        return c

    def kept_now(self, c):
        c.wait()
        self.kept = [k for k in self.kept if k is not c]

    def drain(self):
        for c in self.kept:
            c.wait()
        for c in self.sent:
            c.wait_send()


def barrier(devices):
    sem = pltpu.get_barrier_semaphore()
    for dev in devices:
        pl.semaphore_signal(sem, inc=1, device_id=dev, device_id_type=MESH)
    pl.semaphore_wait(sem, len(devices))


def columns(index, width):
    return pl.ds(pl.multiple_of(index * width, 128), width)


class Ring:
    def __init__(self, cp, to, own, place):
        self.cp, self.to, self.own, self.place = cp, to, own, place

    def start(self):
        send = lambda h, k: self.cp.remote(self.own(h), self.place(0, h), self.to(k))
        self.left0, self.right1 = send(0, 1), send(1, -1)
        self.left1, self.right0 = send(1, 1), send(0, -1)

    def start_half(self, h):
        send = lambda k: self.cp.remote(self.own(h), self.place(0, h), self.to(k))
        if h == 0:
            self.left0, self.right0 = send(1), send(-1)
        else:
            self.right1, self.left1 = send(-1), send(1)

    def turn(self):
        self.left0.wait_recv()
        self.far0 = self.cp.remote(self.place(-1, 0), self.place(-1, 0), self.to(1))
        self.right1.wait_recv()
        self.far1 = self.cp.remote(self.place(1, 1), self.place(1, 1), self.to(-1))

    def near(self):
        self.left1.wait_recv()
        self.right0.wait_recv()

    def far(self):
        self.far0.wait_recv()
        self.far1.wait_recv()


def dot(a, b):
    return jnp.dot(a, b, preferred_element_type=F32)


def distill(
    factor,
    h, d, s, w, p,
    ow, op,
    hh, dd, ss, tt, ww, pp, part, theirs, came, racc, rest,
    gx, gp, gw, rx, sx, rz, rw, sw, rh, tw, tp,
    send, recv, local,
):
    me = Place()
    cp = Copies(send, recv, local)
    sibling, across, beside = me.dev(dc=1), me.dev(dh=1), me.dev(dx=1)
    to_y, to_z = lambda k: me.dev(dy=k), lambda k: me.dev(dz=k)
    barrier(
        [to_y(k) for k in (1, 3, 2)] + [to_z(k) for k in (1, 3, 2)] + [sibling, across, beside]
    )

    piece = me.z * 2 + me.core
    wide = lambda k: columns(lax.rem(me.y + k, 4), 1280)
    rows = pl.ds(pl.multiple_of(piece * 112, 16), 112)
    handed = [[], []]
    for i in (0, 1):
        for k in (2, 1, 3):
            half = columns(lax.rem(me.y + k, 4) * 2 + i, 640)
            to = dd.at[4 - k, piece, :, pl.ds(i * 640, 640)]
            handed[i].append(cp.remote(d.at[rows, half], to, to_y(k)))
    at_hidden = lambda k: columns(lax.rem(me.y + k + 4, 4), 896)
    hidden = Ring(
        cp,
        to_y,
        lambda i: h.at[pl.ds(i * 256, 256)],
        lambda k, i: hh.at[pl.ds(i * 256, 256), at_hidden(k)],
    )

    s_rows = lambda b: pl.ds(pl.multiple_of((me.core * 8 + b) * 64, 64), 64)

    def student_ring(dx):
        def place(k, i):
            return ss.at[s_rows(me.tensor(dy=k, dx=dx)), pl.ds(i * 2048, 2048)]

        own = (lambda i: place(0, i)) if dx else (lambda i: s.at[:, pl.ds(i * 2048, 2048)])
        return Ring(cp, to_y, own, place)

    student, student_beside = student_ring(0), student_ring(1)
    student_x = cp.remote(s, ss.at[s_rows(me.t)], beside)
    student_side = [cp.remote(s, ss.at[s_rows(me.t)], sibling)]

    def student_over_core(k, dx):
        block = ss.at[s_rows(me.tensor(dy=k, dx=dx))]
        student_side.append(cp.remote(block, block, sibling))

    mine, other = columns(me.core, 256), columns(1 - me.core, 256)
    weights = ((w, ww, 256), (p, pp, 320))
    at = lambda q, c, n: pl.ds(pl.multiple_of((q * 2 + c) * n, 64), n)
    pair = lambda q, n: pl.ds(pl.multiple_of(q * 2 * n, 128), 2 * n)
    swap = [
        cp.remote(a.at[:, other], b.at[at(me.q, me.core, n)], sibling) for a, b, n in weights
    ]
    own_weights = [cp.keep(a.at[:, mine], b.at[at(me.q, me.core, n)]) for a, b, n in weights]

    own_teacher = [cp.keep(h, hh.at[:, at_hidden(0)])]
    for i in range(8):
        own_teacher.append(cp.keep(d.at[pl.ds(i * 112, 112), wide(0)], dd.at[0, i]))
    own_student = cp.keep(s, ss.at[s_rows(me.t)])

    for c in own_weights:
        cp.kept_now(c)
    for c in swap:
        c.wait_recv()

    def ring(ref, n, dh):
        block = lambda k, i: ref.at[at(me.chip(dz=k, dh=dh), i, n)]
        return Ring(cp, to_z, lambda i: block(0, i), block)

    weight_rings = [ring(b, n, 0) for a, b, n in weights]
    far_rings = [ring(b, n, 1) for a, b, n in weights]
    far_weights = [
        cp.remote(b.at[pair(me.q, n)], b.at[pair(me.q, n)], across) for a, b, n in weights
    ]
    there = lambda k: lax.rem(me.z + k + 4, 4) * 2 + me.core
    over = lambda k, i: dd.at[1:4, there(k), :, pl.ds(i * 640, 640)]
    down = Ring(cp, to_z, lambda i: over(0, i), over)
    for c in handed[0]:
        c.wait_recv()
    down.start_half(0)
    hidden.start()
    for c in handed[1]:
        c.wait_recv()
    down.start_half(1)
    down_side = []

    def pass_down(k):
        block = dd.at[1:4, there(k)]
        down_side.append(cp.remote(block, block, sibling))

    pass_down(0)

    def teacher_block(out, dx, j):
        left = hh[:, columns(lax.rem(me.y + j, 4), 896)]
        for n in ((0, 256), (256, 256), (512, 128)):
            at_n = pl.ds(pl.multiple_of(lax.rem(me.xl + dx, 2) * 640 + n[0], 128), n[1])
            right = dd[j, :, :, at_n].reshape(896, n[1])
            to = slice(n[0], n[0] + n[1])
            if isinstance(j, int):
                out[:, to] = dot(left, right)
            else:
                out[:, to] += dot(left, right)

    for c in own_teacher:
        cp.kept_now(c)
    teacher_block(theirs, 1, 0)
    teacher_block(part, 0, 0)

    down.turn()
    hidden.turn()
    down.near()
    pass_down(1)
    pass_down(-1)
    down.far()
    pass_down(2)
    for r in weight_rings:
        r.start()
    student_x.wait_recv()
    student.start()
    student_beside.start()
    hidden.near()
    hidden.far()
    for c in down_side:
        c.wait_recv()

    @pl.loop(1, 4)
    def _(j):
        teacher_block(theirs, 1, j)

    chunk = lambda r: pl.ds(r * STEP, STEP)
    partial = [cp.remote(theirs.at[chunk(r)], came.at[chunk(r)], beside) for r in range(STEPS)]

    @pl.loop(1, 4)
    def _(j):
        teacher_block(part, 0, j)

    base = me.core * 512

    def t_block(r, k, dx, i=None):
        n = STEP if i is None else STEP // 2
        row = pl.multiple_of(base + r * STEP + (i or 0) * n, 16)
        return tt.at[pl.ds(row, n), columns(me.tensor(dy=k, dx=dx), 640)]

    def teacher_ring(r, dx):
        place = lambda k, i: t_block(r, k, dx, i)
        return Ring(cp, to_y, lambda i: place(0, i), place)

    rings = [[teacher_ring(r, dx) for dx in (0, 1)] for r in range(STEPS)]
    over_x = {}
    side = [[] for r in range(STEPS)]

    def over_core(r, k, dx):
        side[r].append(cp.remote(t_block(r, k, dx), t_block(r, k, dx), sibling))

    def summed(r):
        partial[r].wait_recv()
        t_block(r, 0, 0)[...] = (part[chunk(r), :] + came[chunk(r), :]).astype(BF16)
        over_x[r] = cp.remote(t_block(r, 0, 0), t_block(r, 0, 0), beside)
        rings[r][0].start()
        over_core(r, 0, 0)

    def exchanged(r):
        over_x[r].wait_recv()
        rings[r][1].start()
        over_core(r, 0, 1)

    def arrived(r):
        for dx in (0, 1):
            rings[r][dx].near()
            over_core(r, 1, dx)
            over_core(r, -1, dx)
            rings[r][dx].far()
            over_core(r, 2, dx)

    def student_output():
        for dx, r in ((0, student), (1, student_beside)):
            r.near()
            r.far()
            for k in (1, -1, 2):
                student_over_core(k, dx)
        student_over_core(0, 1)
        for r in weight_rings + far_rings:
            r.near()
            r.far()
        cp.kept_now(own_student)
        for c in student_side:
            c.wait_recv()

        @pl.loop(0, 4)
        def _(k):
            rows = pl.ds(pl.multiple_of(k * 256, 256), 256)
            racc[rows, :] = dot(ss[rows, :], ww[...])

    def residual(r):
        for c in side[r]:
            c.wait_recv()
        both = [slice(c * 512 + r * STEP, c * 512 + (r + 1) * STEP) for c in (0, 1)]
        target = dot(jnp.concatenate([tt[rows, :] for rows in both], axis=0), pp[...])
        for c, rows in enumerate(both):
            value = racc[rows, :] - target[c * STEP : (c + 1) * STEP, :]
            rest[:, rows] = value.T.astype(BF16)

    for step in range(STEPS + 3):
        if step < STEPS:
            summed(step)
        if 1 <= step <= STEPS:
            exchanged(step - 1)
            rings[step - 1][0].turn()
        if 2 <= step < STEPS + 2:
            rings[step - 2][1].turn()
        if step == 0:
            student.turn()
            student_beside.turn()
            for r in weight_rings:
                r.turn()
            for c, r in zip(far_weights, far_rings):
                c.wait_recv()
                r.start()
        if step == 2:
            for r in far_rings:
                r.turn()
        if step >= 3:
            arrived(step - 3)
        if step == STEPS:
            student_output()
        if step > STEPS:
            residual(step - STEPS - 1)
    for r in range(2, STEPS):
        residual(r)

    def project(**to):
        return dot(rest[...], tt[:, columns(me.chip(**to), 640)])

    def weigh(**to):
        return dot(rest[...], ss[:, columns(me.chip(**to), 512)])

    from_x, from_z = {}, {}
    for k in (2, 1, 3, 0):
        gx[k] = project(dz=k, dh=1).astype(BF16)
        from_x[k] = cp.remote(gx.at[k], rx.at[k], across)
    for g in (1, 0):
        for k in (2, 1, 3):
            gw[g, k] = weigh(dz=k, dh=g).astype(BF16)
            from_z[g, k] = cp.remote(gw.at[g, k], rw.at[g, k - 1], me.dev(dz=k))
    second = {}
    for k in (2, 1, 3):
        gp[...] = project(dz=k)
        from_x[k].wait_recv()
        sx[k - 1] = (gp[...] + rx[k].astype(F32)).astype(BF16)
        second[k] = cp.remote(sx.at[k - 1], rz.at[k - 1], me.dev(dz=k))
    gp[:, :512] = weigh(dh=1)
    for k in (2, 1, 3):
        from_z[1, k].wait_recv()
    sw[...] = (
        gp[:, :512] + rw[1, 0].astype(F32) + rw[1, 1].astype(F32) + rw[1, 2].astype(F32)
    ).astype(BF16)
    back = cp.remote(sw, rh, across)
    last = []

    def hand_out(staged, out, n, parts):
        for i in range(n // 64):
            block = slice(i * 128, i * 128 + 128)
            value = gp[:, block]
            for r in parts:
                value += r[:, block].astype(F32)
            staged[block, :] = (value * factor).T
        theirs = pl.ds(pl.multiple_of((1 - me.core) * n, 64), n)
        ours = pl.ds(pl.multiple_of(me.core * n, 64), n)
        last.append(cp.remote(staged.at[theirs], out.at[:, mine], sibling))
        cp.keep(staged.at[ours], out.at[:, mine])

    gp[...] = project()
    from_x[0].wait_recv()
    for k in (2, 1, 3):
        second[k].wait_recv()
    hand_out(tp, op, 320, [rx.at[0]] + [rz.at[k] for k in range(3)])
    gp[:, :512] = weigh()
    for k in (2, 1, 3):
        from_z[0, k].wait_recv()
    back.wait_recv()
    hand_out(tw, ow, 256, [rw.at[0, k] for k in range(3)] + [rh])
    for c in last:
        c.wait_recv()
    cp.drain()


def on_device(*args):
    narrow = lambda *shape: pltpu.VMEM(shape, BF16)
    wide = lambda *shape: pltpu.VMEM(shape, F32)
    return tuple(
        pl.pallas_call(
            functools.partial(distill, 1.0 / math.sqrt(8192)),
            out_shape=[
                jax.ShapeDtypeStruct((256, 512), F32),
                jax.ShapeDtypeStruct((320, 512), F32),
            ],
            in_specs=[pl.BlockSpec(memory_space=pl.ANY)] * 5,
            out_specs=[pl.BlockSpec(memory_space=pltpu.VMEM)] * 2,
            scratch_shapes=[
                narrow(512, 3584),
                narrow(4, 8, 112, 1280),
                narrow(1024, 4096),
                narrow(1024, 5120),
                narrow(4096, 256),
                narrow(5120, 256),
                wide(512, 640),
                wide(512, 640),
                wide(512, 640),
                wide(1024, 256),
                narrow(256, 1024),
                narrow(4, 256, 640),
                wide(256, 640),
                narrow(2, 4, 256, 512),
                narrow(4, 256, 640),
                narrow(3, 256, 640),
                narrow(3, 256, 640),
                narrow(2, 3, 256, 512),
                narrow(256, 512),
                narrow(256, 512),
                wide(512, 256),
                wide(640, 256),
                pltpu.SemaphoreType.DMA((COPIES,)),
                pltpu.SemaphoreType.DMA((COPIES,)),
                pltpu.SemaphoreType.DMA((16,)),
            ],
            compiler_params=pltpu.CompilerParams(
                collective_id=1, has_side_effects=True, vmem_limit_bytes=VMEM_MIB * 2**20
            ),
        )(*args)
    )


def solution(mesh):
    in_specs = (
        P("dp", "tensor"),
        P("tensor", None),
        P(("dp", "tensor"), None),
        P("dp", "tensor"),
        P("dp", "tensor"),
    )
    out_specs = (P("dp", "tensor"), P("dp", "tensor"))

    return jax.shard_map(
        on_device, mesh=mesh, in_specs=in_specs, out_specs=out_specs, check_vma=False
    )
```

time: 202 us -> 190 us (0.941)
  Pallas kernels: 198 us -> 185 us
    pallas_call x1, Pallas kernels: 198 us -> 185 us  [on_device(): pl.pallas_call(functools.partial(distill, 1.0 / math.sqrt(8192)), out_sha...]
where the time goes in v4:
time: 190 us; the launch traced here: 189 us
  Pallas kernels  185 us (97%)
  local copies, waits for them, and re-layouts  3.84 us (2%)
    pallas_call x1, Pallas kernels, on_device(): pl.pallas_call(functools.partial(distill, 1.0 / math.sqrt(8192)), out_sha...  185 us
    unnamed x2, local copies, waits for them, and re-layouts  3.84 us

profile of v4, /device:TPU:1, one launch (start us, length us, event | category | flops | bytes accessed | tf_op | source)
XLA Modules:
  0.0 189.4 jit_solution(10168350427978702527)
XLA Ops:
  0.6 184.9 %shard_map.68 = (f32[256,512]{1,0:T(8,128)}, f32[320,512]{1,0:T(8,128)}) custom-call(bf16[512,896]{1,0:T(8,128)(2,1)} %h.1, bf16[896,5120]{1,0:T(8,128)(2,1)} %d.1, bf16[64,4096]{1,0:T(8,128)(2,1)} %s.1, bf16[256,512]{1,0:T(8,128)(2,1)} %w.1, bf16[320,512]{1,0:T(8,128)(2,1)} %p.1), custom_call_target="tpu_custom_call" | custom-call | tf_op jit(solution)/shard_map/pallas_call | solution.py:425
  185.5 1.9 copy.9
  187.4 2.0 %copy.10 = f32[320,512]{1,0:T(8,128)} copy(f32[320,512]{1,0:T(8,128)} %get-tuple-element.5) | data formatting | bytes 1310720

commit v5 on v4

--- a/solution.py
+++ b/solution.py
@@ -124,6 +124,38 @@
         self.far1.wait_recv()
 
 
+class RingSum:
+    def __init__(self, cp, to, own, via, came, n):
+        self.cp, self.to, self.own, self.via, self.came = cp, to, own, via, came
+        self.half = (pl.ds(0, n // 2), pl.ds(n // 2, n // 2))
+
+    def begin(self, value):
+        own, half, to, cp = self.own, self.half, self.to, self.cp
+        own[1] = value(2).astype(BF16)
+        self.relayed = [
+            cp.remote(own.at[1, half[0]], self.via.at[0], to(1)),
+            cp.remote(own.at[1, half[1]], self.via.at[1], to(-1)),
+        ]
+        own[0] = value(1).astype(BF16)
+        self.last = [cp.remote(own.at[0, half[1]], self.came.at[0, half[1]], to(1))]
+        own[2] = value(3).astype(BF16)
+        self.last.append(cp.remote(own.at[2, half[0]], self.came.at[1, half[0]], to(-1)))
+
+    def relay(self):
+        for i, (slot, k) in enumerate(((0, 1), (2, -1))):
+            part = self.half[i]
+            self.relayed[i].wait_recv()
+            mine = self.own[slot, part, :].astype(F32)
+            self.own[slot, part, :] = (mine + self.via[i].astype(F32)).astype(BF16)
+            self.last.append(
+                self.cp.remote(self.own.at[slot, part], self.came.at[i, part], self.to(k))
+            )
+
+    def finish(self):
+        for c in self.last:
+            c.wait_recv()
+
+
 def dot(a, b):
     return jnp.dot(a, b, preferred_element_type=F32)
 
@@ -133,7 +165,7 @@
     h, d, s, w, p,
     ow, op,
     hh, dd, ss, tt, ww, pp, part, theirs, came, racc, rest,
-    gx, gp, gw, rx, sx, rz, rw, sw, rh, tw, tp,
+    gx, rx, gp, own_p, via_p, came_p, own_w, via_w, came_w, sw, rh, tw, tp,
     send, recv, local,
 ):
     me = Place()
@@ -141,7 +173,7 @@
     sibling, across, beside = me.dev(dc=1), me.dev(dh=1), me.dev(dx=1)
     to_y, to_z = lambda k: me.dev(dy=k), lambda k: me.dev(dz=k)
     barrier(
-        [to_y(k) for k in (1, 3, 2)] + [to_z(k) for k in (1, 3, 2)] + [sibling, across, beside]
+        [to_y(k) for k in (1, 3, 2)] + [to_z(1), to_z(-1)] + [sibling, across, beside]
     )
 
     piece = me.z * 2 + me.core
@@ -368,27 +400,32 @@
     def weigh(**to):
         return dot(rest[...], ss[:, columns(me.chip(**to), 512)])
 
-    from_x, from_z = {}, {}
+    from_x = {}
     for k in (2, 1, 3, 0):
-        gx[k] = project(dz=k, dh=1).astype(BF16)
+        gx[k] = weigh(dz=k, dh=1).astype(BF16)
         from_x[k] = cp.remote(gx.at[k], rx.at[k], across)
-    for g in (1, 0):
-        for k in (2, 1, 3):
-            gw[g, k] = weigh(dz=k, dh=g).astype(BF16)
-            from_z[g, k] = cp.remote(gw.at[g, k], rw.at[g, k - 1], me.dev(dz=k))
-    second = {}
-    for k in (2, 1, 3):
-        gp[...] = project(dz=k)
+    far_sum, near_sum = [
+        RingSum(cp, to_z, own_p.at[i], via_p.at[i], came_p.at[i], 256) for i in (0, 1)
+    ]
+    weight_sum = RingSum(cp, to_z, own_w, via_w, came_w, 256)
+    far_sum.begin(lambda k: project(dz=k, dh=1))
+    near_sum.begin(lambda k: project(dz=k))
+
+    def crossed(k):
+        value = weigh(dz=k)
         from_x[k].wait_recv()
-        sx[k - 1] = (gp[...] + rx[k].astype(F32)).astype(BF16)
-        second[k] = cp.remote(sx.at[k - 1], rz.at[k - 1], me.dev(dz=k))
-    gp[:, :512] = weigh(dh=1)
-    for k in (2, 1, 3):
-        from_z[1, k].wait_recv()
+        return value + rx[k].astype(F32)
+
+    far_sum.relay()
+    weight_sum.begin(crossed)
+    near_sum.relay()
+    gp[...] = project(dh=1)
+    far_sum.finish()
     sw[...] = (
-        gp[:, :512] + rw[1, 0].astype(F32) + rw[1, 1].astype(F32) + rw[1, 2].astype(F32)
+        gp[...] + came_p[0, 0].astype(F32) + came_p[0, 1].astype(F32)
     ).astype(BF16)
     back = cp.remote(sw, rh, across)
+    weight_sum.relay()
     last = []
 
     def hand_out(staged, out, n, parts):
@@ -403,16 +440,14 @@
         last.append(cp.remote(staged.at[theirs], out.at[:, mine], sibling))
         cp.keep(staged.at[ours], out.at[:, mine])
 
+    gp[:, :512] = weigh()
+    from_x[0].wait_recv()
+    weight_sum.finish()
+    hand_out(tw, ow, 256, [rx.at[0], came_w.at[0], came_w.at[1]])
     gp[...] = project()
-    from_x[0].wait_recv()
-    for k in (2, 1, 3):
-        second[k].wait_recv()
-    hand_out(tp, op, 320, [rx.at[0]] + [rz.at[k] for k in range(3)])
-    gp[:, :512] = weigh()
-    for k in (2, 1, 3):
-        from_z[0, k].wait_recv()
+    near_sum.finish()
     back.wait_recv()
-    hand_out(tw, ow, 256, [rw.at[0, k] for k in range(3)] + [rh])
+    hand_out(tp, op, 320, [came_p.at[1, 0], came_p.at[1, 1], rh])
     for c in last:
         c.wait_recv()
     cp.drain()
@@ -442,15 +477,17 @@
                 wide(512, 640),
                 wide(1024, 256),
                 narrow(256, 1024),
-                narrow(4, 256, 640),
+                narrow(4, 256, 512),
+                narrow(4, 256, 512),
                 wide(256, 640),
-                narrow(2, 4, 256, 512),
-                narrow(4, 256, 640),
-                narrow(3, 256, 640),
-                narrow(3, 256, 640),
-                narrow(2, 3, 256, 512),
-                narrow(256, 512),
-                narrow(256, 512),
+                narrow(2, 3, 256, 640),
+                narrow(2, 2, 128, 640),
+                narrow(2, 2, 256, 640),
+                narrow(3, 256, 512),
+                narrow(2, 128, 512),
+                narrow(2, 256, 512),
+                narrow(256, 640),
+                narrow(256, 640),
                 wide(512, 256),
                 wide(640, 256),
                 pltpu.SemaphoreType.DMA((COPIES,)),

time: 190 us -> 182 us (0.958)
  Pallas kernels: 185 us -> 177 us
    pallas_call x1, Pallas kernels: 185 us -> 177 us  [on_device(): pl.pallas_call(functools.partial(distill, 1.0 / math.sqrt(8192)), out_sha...]
where the time goes in v5:
time: 182 us
  Pallas kernels  177 us (97%)
  local copies, waits for them, and re-layouts  3.84 us (2%)
    pallas_call x1, Pallas kernels, on_device(): pl.pallas_call(functools.partial(distill, 1.0 / math.sqrt(8192)), out_sha...  177 us
    unnamed x2, local copies, waits for them, and re-layouts  3.84 us

profile of v5, /device:TPU:1, one launch (start us, length us, event | category | flops | bytes accessed | tf_op | source)
XLA Modules:
  0.0 181.5 jit_solution(12086584414982535526)
XLA Ops:
  0.6 177.1 %shard_map.68 = (f32[256,512]{1,0:T(8,128)}, f32[320,512]{1,0:T(8,128)}) custom-call(bf16[512,896]{1,0:T(8,128)(2,1)} %h.1, bf16[896,5120]{1,0:T(8,128)(2,1)} %d.1, bf16[64,4096]{1,0:T(8,128)(2,1)} %s.1, bf16[256,512]{1,0:T(8,128)(2,1)} %w.1, bf16[320,512]{1,0:T(8,128)(2,1)} %p.1), custom_call_target="tpu_custom_call" | custom-call | tf_op jit(solution)/shard_map/pallas_call | solution.py:460
  177.7 1.9 %copy.9 = f32[256,512]{1,0:T(8,128)} copy(f32[256,512]{1,0:T(8,128)} %get-tuple-element.4) | data formatting | bytes 1048576
  179.6 2.0 %copy.10 = f32[320,512]{1,0:T(8,128)} copy(f32[320,512]{1,0:T(8,128)} %get-tuple-element.5) | data formatting | bytes 1310720

commit v6 on v5

--- a/solution.py
+++ b/solution.py
@@ -387,7 +387,7 @@
                 r.turn()
         if step >= 3:
             arrived(step - 3)
-        if step == STEPS:
+        if step == STEPS - 1:
             student_output()
         if step > STEPS:
             residual(step - STEPS - 1)
@@ -453,18 +453,20 @@
     cp.drain()
 
 
+def hand_over(gw, gp, ow, op):
+    ow[...] = gw[...]
+    op[...] = gp[...]
+
+
 def on_device(*args):
     narrow = lambda *shape: pltpu.VMEM(shape, BF16)
     wide = lambda *shape: pltpu.VMEM(shape, F32)
-    return tuple(
-        pl.pallas_call(
+    shapes = [jax.ShapeDtypeStruct((rows, 512), F32) for rows in (256, 320)]
+    grads = pl.pallas_call(
             functools.partial(distill, 1.0 / math.sqrt(8192)),
-            out_shape=[
-                jax.ShapeDtypeStruct((256, 512), F32),
-                jax.ShapeDtypeStruct((320, 512), F32),
-            ],
+            out_shape=shapes,
             in_specs=[pl.BlockSpec(memory_space=pl.ANY)] * 5,
-            out_specs=[pl.BlockSpec(memory_space=pltpu.VMEM)] * 2,
+            out_specs=[pl.BlockSpec(memory_space=pl.ANY)] * 2,
             scratch_shapes=[
                 narrow(512, 3584),
                 narrow(4, 8, 112, 1280),
@@ -497,7 +499,14 @@
             compiler_params=pltpu.CompilerParams(
                 collective_id=1, has_side_effects=True, vmem_limit_bytes=VMEM_MIB * 2**20
             ),
-        )(*args)
+    )(*args)
+    return tuple(
+        pl.pallas_call(
+            hand_over,
+            out_shape=shapes,
+            in_specs=[pl.BlockSpec(memory_space=pltpu.VMEM)] * 2,
+            out_specs=[pl.BlockSpec(memory_space=pltpu.VMEM)] * 2,
+        )(*grads)
     )
 
 

time: 182 us -> 177 us (0.973)
  local copies, waits for them, and re-layouts: 3.84 us -> 0 us
    unnamed x2 -> x0, local copies, waits for them, and re-layouts: 3.84 us -> none
    pallas_call x1, Pallas kernels: 177 us -> 173 us  [on_device(): pl.pallas_call(functools.partial(distill, 1.0 / math.sqrt(8192)), out_sha...]
    pallas_call x0 -> x1, Pallas kernels: none -> 2.29 us  [on_device(): pl.pallas_call(hand_over, out_shape=shapes, in_specs=[pl.BlockSpec(memory...]
where the time goes in v6:
time: 177 us; the launch traced here: 176 us
  Pallas kernels  176 us (99%)
    pallas_call x1, Pallas kernels, on_device(): pl.pallas_call(functools.partial(distill, 1.0 / math.sqrt(8192)), out_sha...  173 us

profile of v6, /device:TPU:1, one launch (start us, length us, event | category | flops | bytes accessed | tf_op | source)
XLA Modules:
  0.0 176.4 jit_solution(7168923175069009362)
XLA Ops:
  0.6 173.4 %shard_map.68 = (f32[256,512]{1,0:T(8,128)}, f32[320,512]{1,0:T(8,128)}) custom-call(bf16[512,896]{1,0:T(8,128)(2,1)} %h.1, bf16[896,5120]{1,0:T(8,128)(2,1)} %d.1, bf16[64,4096]{1,0:T(8,128)(2,1)} %s.1, bf16[256,512]{1,0:T(8,128)(2,1)} %w.1, bf16[320,512]{1,0:T(8,128)(2,1)} %p.1), custom_call_target="tpu_custom_call" | custom-call | tf_op jit(solution)/shard_map/pallas_call | solution.py:465
  174.1 2.3 %shard_map.69 = (f32[256,512]{1,0:T(8,128)}, f32[320,512]{1,0:T(8,128)}) custom-call(f32[256,512]{1,0:T(8,128)} %get-tuple-element.4.gw, f32[320,512]{1,0:T(8,128)} %get-tuple-element.5.gp), custom_call_target="tpu_custom_call" | custom-call | tf_op jit(solution)/shard_map/pallas_call | solution.py:504

commit v7 on v6

--- a/solution.py
+++ b/solution.py
@@ -387,7 +387,7 @@
                 r.turn()
         if step >= 3:
             arrived(step - 3)
-        if step == STEPS - 1:
+        if step == STEPS - 2:
             student_output()
         if step > STEPS:
             residual(step - STEPS - 1)
@@ -401,14 +401,19 @@
         return dot(rest[...], ss[:, columns(me.chip(**to), 512)])
 
     from_x = {}
-    for k in (2, 1, 3, 0):
+
+    def cross(k):
         gx[k] = weigh(dz=k, dh=1).astype(BF16)
         from_x[k] = cp.remote(gx.at[k], rx.at[k], across)
+
+    cross(2)
     far_sum, near_sum = [
         RingSum(cp, to_z, own_p.at[i], via_p.at[i], came_p.at[i], 256) for i in (0, 1)
     ]
     weight_sum = RingSum(cp, to_z, own_w, via_w, came_w, 256)
     far_sum.begin(lambda k: project(dz=k, dh=1))
+    for k in (1, 3, 0):
+        cross(k)
     near_sum.begin(lambda k: project(dz=k))
 
     def crossed(k):

time: 177 us -> 175 us (0.989)
  no operation moved by 1% of the time
where the time goes in v7:
time: 175 us
  Pallas kernels  175 us (100%)
    pallas_call x1, Pallas kernels, on_device(): pl.pallas_call(functools.partial(distill, 1.0 / math.sqrt(8192)), out_sha...  172 us

profile of v7, /device:TPU:1, one launch (start us, length us, event | category | flops | bytes accessed | tf_op | source)
XLA Modules:
  0.0 175.2 jit_solution(10535701873535395942)
XLA Ops:
  0.6 172.2 %shard_map.68 = (f32[256,512]{1,0:T(8,128)}, f32[320,512]{1,0:T(8,128)}) custom-call(bf16[512,896]{1,0:T(8,128)(2,1)} %h.1, bf16[896,5120]{1,0:T(8,128)(2,1)} %d.1, bf16[64,4096]{1,0:T(8,128)(2,1)} %s.1, bf16[256,512]{1,0:T(8,128)(2,1)} %w.1, bf16[320,512]{1,0:T(8,128)(2,1)} %p.1), custom_call_target="tpu_custom_call" | custom-call | tf_op jit(solution)/shard_map/pallas_call | solution.py:470
  172.9 2.3 %shard_map.69 = (f32[256,512]{1,0:T(8,128)}, f32[320,512]{1,0:T(8,128)}) custom-call(f32[256,512]{1,0:T(8,128)} %get-tuple-element.4.gw, f32[320,512]{1,0:T(8,128)} %get-tuple-element.5.gp), custom_call_target="tpu_custom_call" | custom-call | tf_op jit(solution)/shard_map/pallas_call | solution.py:509
